TPU v7x, 256 devices: a whole 4x4x8 slice. The times are simulated.
256 devices in a mesh: energy: 64 (over z, y_lo, x), cuts: 4 (over y_hi, core).
Axes of the slice: x: 4, y: 4 (y_hi: 2, y_lo: 2; y = y_hi * 2 + y_lo), z: 8, core: 2. Of those that a mesh axis runs over, the one named last changes fastest.
Arguments:
- lesser: bfloat16 [128, 4, 2, 512, 512], P('energy', 'cuts'), may hold values from -6 to 6
- greater: bfloat16 [128, 4, 2, 512, 512], P('energy', 'cuts'), may hold values from -6 to 6
- couplings: bfloat16 [4, 3, 512, 512], P('cuts'), may hold values from -0.25 to 0.25
- rim_couple: bfloat16 [4, 2, 128, 128], P('cuts'), may hold values from -0.5 to 0.5
- bose_factor: float32 [3], replicated, may hold values from 0.05 to 2
- offsets: int32 [3], replicated, may hold values from 1 to 2, as said below
- pattern: int32 [4, 3], replicated, may hold values from 0 to 1, as said below
Outputs:
- sigma_lesser: bfloat16 [128, 4, 2, 512, 512], P('energy', 'cuts')
- sigma_retarded: bfloat16 [128, 4, 2, 512, 512], P('energy', 'cuts')
Inputs may be any that keep to these rules, and one draw needn't show every extreme that they name: `offsets`: one mode's shift is exactly 2. `pattern`: each block couples to 1 to 3 modes. In every draw one block couples to all 3 modes and the other block of its aligned pair (blocks 2i and 2i + 1) to exactly one.
All inputs are finite; a program needn't handle non-finite values.
Results may differ from a plain program's by a relative error of at most 0.0057.
Values may be sent and summed in bfloat16 or wider, within the bound.
No kernel may reach another device: no remote copies, remote signals or barrier semaphores. Data moves between devices by JAX's collectives and lax.ppermute only.
A program may use at most 128 MiB of HBM per device.

v0:
```python
import jax
import jax.numpy as jnp
from jax import lax
from jax.experimental import pallas as pl
from jax.experimental.pallas import tpu as pltpu
from jax.sharding import PartitionSpec as P


def shifted(x, energies, cuts, first):
    pairs = []
    for e in range(energies):
        for c in range(cuts):
            up = (c % 2 == 0) == first
            to = e + 1 if up else e - 1
            if 0 <= to < energies:
                pairs.append((e * cuts + c, to * cuts + c))
    return lax.ppermute(x, ("energy", "cuts"), pairs)


def swapped(x, energies, cuts, inside):
    pairs = []
    for e in range(energies):
        for c in range(cuts):
            to = c ^ 1 if inside else (c + 1 if c % 2 else c - 1)
            if 0 <= to < cuts:
                pairs.append((e * cuts + c, e * cuts + to))
    return lax.ppermute(x, ("energy", "cuts"), pairs)


def product(a, b):
    return lax.dot_general(a, b, (((1,), (0,)), ((), ())), preferred_element_type=jnp.float32)


def product_t(a, b):
    return lax.dot_general(a, b, (((1,), (1,)), ((), ())), preferred_element_type=jnp.float32)


def call(kernel, name, scalars, operands, grid, in_specs, out_specs, out_shape, vmem, flops, **more):
    scratch = more.pop("scratch", [])
    return pl.pallas_call(
        kernel,
        grid_spec=pltpu.PrefetchScalarGridSpec(
            num_scalar_prefetch=len(scalars),
            grid=grid,
            in_specs=in_specs,
            out_specs=out_specs,
            scratch_shapes=scratch,
        ),
        out_shape=out_shape,
        compiler_params=pltpu.CompilerParams(vmem_limit_bytes=vmem * 2**20),
        cost_estimate=pl.CostEstimate(flops=flops, bytes_accessed=4 * 2**20, transcendentals=0),
        name=name,
        **more,
    )(*scalars, *operands)


def corner_kernel(inside, low_top, high_top, low_bottom, high_bottom, out):
    core = lax.axis_index("cuts") & 1
    for kind, (top, bottom) in enumerate(((low_top, low_bottom), (high_top, high_bottom))):
        upper = core == 1 if inside else core == 0
        out[:, kind] = jnp.where(upper, top[:, 0], bottom[:, 0])


def cornered(inside, width, lesser, greater):
    parts = lesser.shape[2]
    last = lesser.shape[-1] // width - 1
    shape = (2, 2, parts, width, width)
    block = (2, 1, parts, width, width)
    top = pl.BlockSpec(block, lambda i: (0, 0, 0, 0, 0))
    bottom = pl.BlockSpec(block, lambda i: (0, 0, 0, last, last))
    return call(
        lambda *refs: corner_kernel(inside, *refs),
        "cornered",
        (),
        (lesser, greater, lesser, greater),
        (1,),
        [top, top, bottom, bottom],
        pl.BlockSpec(shape, lambda i: (0, 0, 0, 0, 0)),
        jax.ShapeDtypeStruct(shape, lesser.dtype),
        60,
        0,
    )


def place_kernel(out):
    cut = lax.axis_index("cuts")
    out[0] = cut
    out[1] = cut & 1


def placed():
    return call(
        place_kernel,
        "placed",
        (),
        (),
        (),
        [],
        pl.BlockSpec(memory_space=pltpu.SMEM),
        jax.ShapeDtypeStruct((2,), jnp.int32),
        60,
        10**12,
    )


def far_kernel(place, offsets, pattern, bose, green, couple, first_out, second_out, left, total):
    cut, core = place[0], place[1]
    orbitals = couple.shape[-1]
    total[...] = jnp.zeros_like(total)
    for mode in range(couple.shape[1]):

        @pl.when((pattern[cut, mode] > 0) & (offsets[mode] == 2))
        def _():
            matrix = couple[0, mode]
            for energy in range(2):
                weight = bose[mode] + (1.0 if energy == 0 else 0.0)
                rows = slice(energy * orbitals, (energy + 1) * orbitals)
                left[rows] = (product(matrix, green[energy, 0, 0]) * weight).astype(jnp.bfloat16)
            total[...] += product_t(left[...], matrix)

    for slot, out in enumerate((first_out, second_out)):
        start = pl.multiple_of((core if slot == 0 else 1 - core) * orbitals, orbitals)
        out[0] = (0.5 * total[pl.ds(start, orbitals)]).astype(jnp.bfloat16)


def far_terms(scalars, bose, greater, couplings):
    parts, orbitals = greater.shape[2], greater.shape[-1]
    modes = couplings.shape[1]
    whole = pl.BlockSpec((1, orbitals, orbitals), lambda p, *_: (p, 0, 0))
    return call(
        far_kernel,
        "far_terms",
        (*scalars, bose),
        (greater, couplings),
        (parts,),
        [
            pl.BlockSpec((2, 1, 1, orbitals, orbitals), lambda p, *_: (0, 0, p, 0, 0)),
            pl.BlockSpec((1, modes, orbitals, orbitals), lambda p, *_: (0, 0, 0, 0)),
        ],
        [whole, whole],
        [jax.ShapeDtypeStruct((parts, orbitals, orbitals), jnp.bfloat16)] * 2,
        60,
        64 * modes * orbitals**3,
        scratch=[
            pltpu.VMEM((2 * orbitals, orbitals), jnp.bfloat16),
            pltpu.VMEM((2 * orbitals, orbitals), jnp.float32),
        ],
    )


def fetch(part, parts, copies):
    @pl.when(part == 0)
    def _():
        for copy in sum(copies, []):
            copy.start()

    for p in range(parts):

        @pl.when(part == p)
        def _():
            for copy in copies[p]:
                copy.wait()


def add_corners(core, inner, outer, rim, total):
    orbitals, width = total.shape[-1], rim.shape[-1]
    for energy in range(2):
        for side in range(2):
            matrix = rim[0, side]
            corner = jnp.where(core == side, outer[energy, 0, 0], inner[energy, 0, 0])
            left = product(matrix, corner).astype(jnp.bfloat16)
            start = 0 if side == 0 else orbitals - width
            rows = slice(energy * orbitals + start, energy * orbitals + start + width)
            total[rows, start : start + width] += product_t(left, matrix)


def blended(ahead, lead, behind, trail):
    mixed = lead * ahead.astype(jnp.float32) + trail * behind.astype(jnp.float32)
    return mixed.astype(jnp.bfloat16)


def lesser_kernel(
    place, offsets, pattern, bose,
    own, first, second, inner, outer, couple, rim, out, kept, window, left, total, sems,
):
    cut, core = place[0], place[1]
    part = pl.program_id(0)
    orbitals = couple.shape[-1]
    fetch(
        part,
        2,
        [
            [
                pltpu.make_async_copy(own.at[:, 0, p], window.at[p, pl.ds(2, 2)], sems.at[p, 0]),
                pltpu.make_async_copy(
                    first.at[:, 0, p], window.at[p, pl.ds(4 * core, 2)], sems.at[p, 1]
                ),
                pltpu.make_async_copy(
                    second.at[:, 0, p], window.at[p, pl.ds(4 - 4 * core, 2)], sems.at[p, 2]
                ),
            ]
            for p in range(2)
        ],
    )
    here = window.at[part]
    total[...] = jnp.zeros_like(total)
    add_corners(core, inner, outer, rim, total)
    for mode in range(couple.shape[1]):

        @pl.when(pattern[cut, mode] > 0)
        def _():
            shift, matrix = offsets[mode], couple[0, mode]
            for energy in range(2):
                rows = slice(energy * orbitals, (energy + 1) * orbitals)
                mixed = blended(
                    here[2 + energy + shift], bose[mode] + 1.0, here[2 + energy - shift], bose[mode]
                )
                left[rows] = product(matrix, mixed).astype(jnp.bfloat16)
            total[...] += product_t(left[...], matrix)

    for energy in range(2):
        rows = slice(energy * orbitals, (energy + 1) * orbitals)
        out[energy, 0, 0] = total[rows].astype(jnp.bfloat16)
        kept[0, energy] = total[rows]


def greater_kernel(
    place, offsets, pattern, bose,
    own, first, second, inner, outer, low, couple, rim, kept, window, left, total, sems,
):
    cut, core = place[0], place[1]
    part = pl.program_id(0)
    orbitals = couple.shape[-1]
    fetch(
        part,
        2,
        [
            [
                pltpu.make_async_copy(own.at[:, 0, p], window.at[p, pl.ds(1, 2)], sems.at[p, 0]),
                pltpu.make_async_copy(first.at[0, 0, p], window.at[p, 3 * core], sems.at[p, 1]),
                pltpu.make_async_copy(second.at[0, 0, p], window.at[p, 3 - 3 * core], sems.at[p, 2]),
            ]
            for p in range(2)
        ],
    )
    here = window.at[part]
    total[...] = jnp.zeros_like(total)
    add_corners(core, inner, outer, rim, total)
    for mode in range(couple.shape[1]):
        active = pattern[cut, mode] > 0

        @pl.when(active & (offsets[mode] == 2))
        def _():
            matrix = couple[0, mode]
            for energy in range(2):
                rows = slice(energy * orbitals, (energy + 1) * orbitals)
                weight = bose[mode] + (0.0 if energy == 0 else 1.0)
                left[rows] = (product(matrix, here[3 - 3 * energy]) * weight).astype(jnp.bfloat16)
            total[...] += product_t(left[...], matrix)

        @pl.when(active & (offsets[mode] != 2))
        def _():
            matrix = couple[0, mode]
            for energy in range(2):
                rows = slice(energy * orbitals, (energy + 1) * orbitals)
                mixed = blended(here[2 + energy], bose[mode], here[energy], bose[mode] + 1.0)
                left[rows] = product(matrix, mixed).astype(jnp.bfloat16)
            total[...] += product_t(left[...], matrix)

    for energy in range(2):
        rows = slice(energy * orbitals, (energy + 1) * orbitals)
        kept[energy, 0, 0] = (0.5 * (total[rows] - low[0, energy])).astype(kept.dtype)


def product_specs(kind, slots, couplings, rim_couple):
    modes, orbitals = couplings.shape[1], couplings.shape[2]
    width = rim_couple.shape[-1]
    corner = pl.BlockSpec((2, 1, 1, width, width), lambda p, *_: (0, kind, p, 0, 0))
    matrices = [
        pl.BlockSpec((1, modes, orbitals, orbitals), lambda p, *_: (0, 0, 0, 0)),
        pl.BlockSpec((1, 2, width, width), lambda p, *_: (0, 0, 0, 0)),
    ]
    scratch = [
        pltpu.VMEM((2, slots, orbitals, orbitals), jnp.bfloat16),
        pltpu.VMEM((2 * orbitals, orbitals), jnp.bfloat16),
        pltpu.VMEM((2 * orbitals, orbitals), jnp.float32),
        pltpu.SemaphoreType.DMA((2, 3)),
    ]
    kept = pl.BlockSpec((1, 2, orbitals, orbitals), lambda p, *_: (p, 0, 0, 0))
    return [pl.BlockSpec(memory_space=pl.ANY)] * 3 + [corner, corner], matrices, kept, scratch


def lesser_terms(scalars, bose, lesser, first, second, corners, couplings, rim_couple):
    parts, orbitals = lesser.shape[2], lesser.shape[-1]
    inputs, matrices, kept, scratch = product_specs(0, 6, couplings, rim_couple)
    return call(
        lesser_kernel,
        "lesser_terms",
        (*scalars, bose),
        (lesser, first, second, *corners, couplings, rim_couple),
        (parts,),
        inputs + matrices,
        [pl.BlockSpec((2, 1, 1, orbitals, orbitals), lambda p, *_: (0, 0, p, 0, 0)), kept],
        [
            jax.ShapeDtypeStruct(lesser.shape, jnp.bfloat16),
            jax.ShapeDtypeStruct((parts, 2, orbitals, orbitals), jnp.float32),
        ],
        60,
        12 * 8 * orbitals**3,
        scratch=scratch,
    )


def greater_terms(scalars, bose, greater, first, second, corners, low, couplings, rim_couple):
    parts, orbitals = greater.shape[2], greater.shape[-1]
    inputs, matrices, kept, scratch = product_specs(1, 4, couplings, rim_couple)
    return call(
        greater_kernel,
        "greater_terms",
        (*scalars, bose),
        (greater, first, second, *corners, low, couplings, rim_couple),
        (parts,),
        inputs + [kept] + matrices,
        pl.BlockSpec((2, 1, 1, orbitals, orbitals), lambda p, *_: (0, 0, p, 0, 0)),
        jax.ShapeDtypeStruct(greater.shape, jnp.bfloat16),
        60,
        12 * 8 * orbitals**3,
        scratch=scratch,
    )


def added(core, near, first, second):
    energy = lax.broadcasted_iota(jnp.int32, near.shape, 0)
    far = jnp.where(energy == core, first[None, None], second[None, None])
    return (near.astype(jnp.float32) + far.astype(jnp.float32)).astype(jnp.bfloat16)


def body(lesser, greater, couplings, rim_couple, bose_factor, offsets, pattern):
    energies = lax.axis_size("energy")
    cuts = lax.axis_size("cuts")
    width = rim_couple.shape[-1]
    core = lax.axis_index("cuts") & 1

    outer = swapped(cornered(False, width, lesser, greater), energies, cuts, False)
    place, lesser_sent = lax.optimization_barrier((placed(), lesser))
    low = [shifted(lesser_sent, energies, cuts, first) for first in (True, False)]
    near = [lax.dynamic_slice_in_dim(greater, at, 1, 0) for at in (1 - core, core)]
    outer, place = lax.optimization_barrier((outer, place))
    high = [shifted(term, energies, cuts, i == 0) for i, term in enumerate(near)]
    scalars = (place, offsets, pattern)

    first, second = far_terms(scalars, bose_factor, greater, couplings)
    second, lesser_corner = lax.optimization_barrier((second, lesser))
    inner = swapped(cornered(True, width, lesser_corner, greater), energies, cuts, True)
    inner, first = lax.optimization_barrier((inner, first))
    corners = (inner, outer)
    first = shifted(first, energies, cuts, True)
    low, second = lax.optimization_barrier((low, second))
    second = shifted(second, energies, cuts, False)

    low_out, low_kept = lesser_terms(
        scalars, bose_factor, lesser, *low, corners, couplings, rim_couple
    )
    kept = greater_terms(
        scalars, bose_factor, greater, *high, corners, low_kept, couplings, rim_couple
    )
    return low_out, added(core, kept, first, second)


def solution(mesh):
    return jax.shard_map(
        body,
        mesh=mesh,
        in_specs=(
            P("energy", "cuts", None, None, None),
            P("energy", "cuts", None, None, None),
            P("cuts", None, None, None),
            P("cuts", None, None, None),
            P(),
            P(),
            P(),
        ),
        out_specs=(P("energy", "cuts", None, None, None), P("energy", "cuts", None, None, None)),
        check_vma=False,
    )
```

profile of v0, /device:TPU:110, one launch (start us, length us, event | category | flops | bytes accessed | tf_op | source)
XLA Modules:
  0.0 110.1 jit_solution(11806861284506930493)
XLA Ops:
  0.6 1.9 %cornered.2 = bf16[2,2,2,128,128]{4,3,2,1,0:T(8,128)(2,1)} custom-call(bf16[2,1,2,512,512]{4,3,2,1,0:T(8,128)(2,1)} %own.2, bf16[2,1,2,512,512]{4,3,2,1,0:T(8,128)(2,1)} %own.3, bf16[2,1,2,512,512]{4,3,2,1,0:T(8,128)(2,1)} %own.2, bf16[2,1,2,512,512]{4,3,2,1,0:T(8,128)(2,1)} %own.3), custom_call_target="tpu_custom_call" | custom-call | bytes 4194304 | tf_op jit(solution)/shard_map/cornered/pallas_call | solution.py:40
  2.5 1.4 %collective-permute-start = (bf16[2,2,2,128,128]{4,3,2,1,0:T(8,128)(2,1)}, bf16[2,2,2,128,128]{4,3,2,1,0:T(8,128)(2,1)}, u32[]{:S(2)}, u32[]{:S(2)}) collective-permute-start(bf16[2,2,2,128,128]{4,3,2,1,0:T(8,128)(2,1)} %cornered.2), channel_id=1, source_target_pairs={{1,2},{2,1},{5,6},{6,5},{9,10},{10,9},{13,14},{14,13},{17,18},{18,... | collective-permute-start | bytes 786440 | tf_op jit(solution)/shard_map/ppermute | solution.py:27
  3.9 0.5 placed.1.place
  4.4 4.8 %collective-permute-start.1 = (bf16[2,1,2,512,512]{4,3,2,1,0:T(8,128)(2,1)}, bf16[2,1,2,512,512]{4,3,2,1,0:T(8,128)(2,1)}, u32[]{:S(2)}, u32[]{:S(2)}) collective-permute-start(bf16[2,1,2,512,512]{4,3,2,1,0:T(8,128)(2,1)} %own.2), channel_id=1, source_target_pairs={{0,4},{2,6},{4,8},{5,1},{6,10},{7,3},{8,12},{9,5},{10,14},{11,7},{... | collective-permute-start | bytes 6291464 | tf_op jit(solution)/shard_map/ppermute | solution.py:17
  9.3 1.9 %collective-permute-start.2 = (bf16[2,1,2,512,512]{4,3,2,1,0:T(8,128)(2,1)}, bf16[2,1,2,512,512]{4,3,2,1,0:T(8,128)(2,1)}, u32[]{:S(2)}, u32[]{:S(2)}) collective-permute-start(bf16[2,1,2,512,512]{4,3,2,1,0:T(8,128)(2,1)} %own.2), channel_id=1, source_target_pairs={{1,5},{3,7},{4,0},{5,9},{6,2},{7,11},{8,4},{9,13},{10,6},{11,15},{... | collective-permute-start | bytes 6291464 | tf_op jit(solution)/shard_map/ppermute | solution.py:17
  11.2 0.0 collective-permute-done.outer
  11.2 9.0 %far_terms.1 = (bf16[2,512,512]{2,1,0:T(8,128)(2,1)}, bf16[2,512,512]{2,1,0:T(8,128)(2,1)}) custom-call(s32[2]{0:T(128)} %placed.1.place, s32[3]{0:T(128)} %offsets.5, s32[4,3]{1,0:T(4,128)} %pattern.5, f32[3]{0:T(128)} %bose.5, bf16[2,1,2,512,512]{4,3,2,1,0:T(8,128)(2,1)} %own.3, bf16[1,3,512,512]{3,2,1,0:T(8,128)(2,1)} %couple.5), custom_call_target="tpu_custom_call" | custom-call | flops 25769803776 | bytes 4194304 | tf_op jit(solution)/shard_map/far_terms/pallas_call | solution.py:40
  20.2 0.0 copy-start
  20.2 2.0 %cornered.3 = bf16[2,2,2,128,128]{4,3,2,1,0:T(8,128)(2,1)} custom-call(bf16[2,1,2,512,512]{4,3,2,1,0:T(8,128)(2,1)} %own.2, bf16[2,1,2,512,512]{4,3,2,1,0:T(8,128)(2,1)} %own.3, bf16[2,1,2,512,512]{4,3,2,1,0:T(8,128)(2,1)} %own.2, bf16[2,1,2,512,512]{4,3,2,1,0:T(8,128)(2,1)} %own.3), custom_call_target="tpu_custom_call" | custom-call | bytes 4194304 | tf_op jit(solution)/shard_map/cornered/pallas_call | solution.py:40
  22.3 8.2 %collective-permute-start.3 = (bf16[2,2,2,128,128]{4,3,2,1,0:T(8,128)(2,1)}, bf16[2,2,2,128,128]{4,3,2,1,0:T(8,128)(2,1)S(1)}, u32[]{:S(2)}, u32[]{:S(2)}) collective-permute-start(bf16[2,2,2,128,128]{4,3,2,1,0:T(8,128)(2,1)} %cornered.3), channel_id=1, source_target_pairs={{0,1},{1,0},{2,3},{3,2},{4,5},{5,4},{6,7},{7,6},{8,9},{9,8},{10,11... | collective-permute-start | bytes 786440 | tf_op jit(solution)/shard_map/ppermute | solution.py:27
  30.4 0.0 copy-done
  30.4 1.1 %constant_dynamic-slice_fusion = (bf16[1,1,2,512,512]{4,3,2,1,0:T(8,128)(2,1)S(1)}, bf16[1,1,2,512,512]{4,3,2,1,0:T(8,128)(2,1)}) fusion(bf16[2,1,2,512,512]{4,3,2,1,0:T(8,128)(2,1)S(1)} %copy-done, s32[]{:T(128)S(6)} %select_n.19, s32[]{:T(128)S(6)} %select_n.18), kind=kLoop, calls=%fused_computation.2 | loop fusion | bytes 4194312 | tf_op jit(solution)/shard_map/dynamic_slice | solution.py:347
  31.5 2.2 %collective-permute-start.4 = (bf16[1,1,2,512,512]{4,3,2,1,0:T(8,128)(2,1)}, bf16[1,1,2,512,512]{4,3,2,1,0:T(8,128)(2,1)}, u32[]{:S(2)}, u32[]{:S(2)}) collective-permute-start(bf16[1,1,2,512,512]{4,3,2,1,0:T(8,128)(2,1)} %get-tuple-element.33), channel_id=1, source_target_pairs={{0,4},{2,6},{4,8},{5,1},{6,10},{7,3},{8,12},{9,5},{10,14},{11,7},{... | collective-permute-start | bytes 3145736 | tf_op jit(solution)/shard_map/ppermute | solution.py:17
  33.7 3.6 %collective-permute-start.5 = (bf16[1,1,2,512,512]{4,3,2,1,0:T(8,128)(2,1)S(1)}, bf16[1,1,2,512,512]{4,3,2,1,0:T(8,128)(2,1)}, u32[]{:S(2)}, u32[]{:S(2)}) collective-permute-start(bf16[1,1,2,512,512]{4,3,2,1,0:T(8,128)(2,1)S(1)} %get-tuple-element.32), channel_id=1, source_target_pairs={{1,5},{3,7},{4,0},{5,9},{6,2},{7,11},{8,4},{9,13},{10,6},{11,15},{... | collective-permute-start | bytes 3145736 | tf_op jit(solution)/shard_map/ppermute | solution.py:17
  37.4 0.0 collective-permute-done.3.inner
  37.4 0.0 copy-start.1
  37.4 6.4 %collective-permute-start.6 = (bf16[2,512,512]{2,1,0:T(8,128)(2,1)}, bf16[2,512,512]{2,1,0:T(8,128)(2,1)S(1)}, u32[]{:S(2)}, u32[]{:S(2)}) collective-permute-start(bf16[2,512,512]{2,1,0:T(8,128)(2,1)} %get-tuple-element.30), channel_id=1, source_target_pairs={{0,4},{2,6},{4,8},{5,1},{6,10},{7,3},{8,12},{9,5},{10,14},{11,7},{... | collective-permute-start | bytes 3145736 | tf_op jit(solution)/shard_map/ppermute | solution.py:17
  43.8 6.8 %collective-permute-done.1.first = bf16[2,1,2,512,512]{4,3,2,1,0:T(8,128)(2,1)} collective-permute-done((bf16[2,1,2,512,512]{4,3,2,1,0:T(8,128)(2,1)}, bf16[2,1,2,512,512]{4,3,2,1,0:T(8,128)(2,1)}, u32[]{:S(2)}, u32[]{:S(2)}) %collective-permute-start.1) | collective-permute-done | bytes 2097184 | tf_op jit(solution)/shard_map/ppermute | solution.py:17
  50.6 13.7 %collective-permute-done.2.second = bf16[2,1,2,512,512]{4,3,2,1,0:T(8,128)(2,1)} collective-permute-done((bf16[2,1,2,512,512]{4,3,2,1,0:T(8,128)(2,1)}, bf16[2,1,2,512,512]{4,3,2,1,0:T(8,128)(2,1)}, u32[]{:S(2)}, u32[]{:S(2)}) %collective-permute-start.2) | collective-permute-done | bytes 2097184 | tf_op jit(solution)/shard_map/ppermute | solution.py:17
  64.3 2.1 %collective-permute-start.7 = (bf16[2,512,512]{2,1,0:T(8,128)(2,1)}, bf16[2,512,512]{2,1,0:T(8,128)(2,1)S(1)}, u32[]{:S(2)}, u32[]{:S(2)}) collective-permute-start(bf16[2,512,512]{2,1,0:T(8,128)(2,1)} %get-tuple-element.31), channel_id=1, source_target_pairs={{1,5},{3,7},{4,0},{5,9},{6,2},{7,11},{8,4},{9,13},{10,6},{11,15},{... | collective-permute-start | bytes 3145736 | tf_op jit(solution)/shard_map/ppermute | solution.py:17
  66.4 0.0 copy-done.1
  66.4 12.6 %lesser_terms.1 = (bf16[2,1,2,512,512]{4,3,2,1,0:T(8,128)(2,1)}, f32[2,2,512,512]{3,2,1,0:T(8,128)}) custom-call(s32[2]{0:T(128)} %placed.1.place, s32[3]{0:T(128)} %offsets.5, s32[4,3]{1,0:T(4,128)} %pattern.5, f32[3]{0:T(128)} %bose.5, bf16[2,1,2,512,512]{4,3,2,1,0:T(8,128)(2,1)} %own.2, bf16[2,1,2,512,512]{4,3,2,1,0:T(8,128)(2,1)} %collective-permute-done.1.first, ...), custom_call_target="tpu_custom_call" | custom-call | flops 12884901888 | bytes 4194304 | tf_op jit(solution)/shard_map/lesser_terms/pallas_call | solution.py:40
  79.0 0.0 collective-permute-done.4.first
  79.0 7.7 %collective-permute-done.5.second = bf16[1,1,2,512,512]{4,3,2,1,0:T(8,128)(2,1)} collective-permute-done((bf16[1,1,2,512,512]{4,3,2,1,0:T(8,128)(2,1)S(1)}, bf16[1,1,2,512,512]{4,3,2,1,0:T(8,128)(2,1)}, u32[]{:S(2)}, u32[]{:S(2)}) %collective-permute-start.5) | collective-permute-done | bytes 1048608 | tf_op jit(solution)/shard_map/ppermute | solution.py:17
  86.7 12.1 %greater_terms.1 = bf16[2,1,2,512,512]{4,3,2,1,0:T(8,128)(2,1)} custom-call(s32[2]{0:T(128)} %placed.1.place, s32[3]{0:T(128)} %offsets.5, s32[4,3]{1,0:T(4,128)} %pattern.5, f32[3]{0:T(128)} %bose.5, bf16[2,1,2,512,512]{4,3,2,1,0:T(8,128)(2,1)} %own.3, bf16[1,1,2,512,512]{4,3,2,1,0:T(8,128)(2,1)} %collective-permute-done.4.first, ...), custom_call_target="tpu_custom_call" | custom-call | flops 12884901888 | bytes 4194304 | tf_op jit(solution)/shard_map/greater_terms/pallas_call | solution.py:40
  98.8 0.0 collective-permute-done.6
  98.8 7.4 %collective-permute-done.7 = bf16[2,512,512]{2,1,0:T(8,128)(2,1)S(1)} collective-permute-done((bf16[2,512,512]{2,1,0:T(8,128)(2,1)}, bf16[2,512,512]{2,1,0:T(8,128)(2,1)S(1)}, u32[]{:S(2)}, u32[]{:S(2)}) %collective-permute-start.7) | collective-permute-done | bytes 1048608 | tf_op jit(solution)/shard_map/ppermute | solution.py:17
  106.2 4.0 %add_convert_fusion = bf16[2,1,2,512,512]{4,3,2,1,0:T(8,128)(2,1)} fusion(bf16[2,1,2,512,512]{4,3,2,1,0:T(8,128)(2,1)} %greater_terms.1, pred[2]{0:T(512)(128)(4,1)S(1)} %iota_compare_fusion, bf16[2,512,512]{2,1,0:T(8,128)(2,1)S(1)} %collective-permute-done.7, bf16[2,512,512]{2,1,0:T(8,128)(2,1)S(1)} %collective-permute-done.6), kind=kLoop, calls=%fused_computation | loop fusion | flops 5242880 | bytes 6291458 | tf_op jit(solution)/shard_map/convert_element_type | solution.py:335
  (1 shorter events, 0.0 us)
Async XLA Ops:
  2.5 8.7 %collective-permute-start = (bf16[2,2,2,128,128]{4,3,2,1,0:T(8,128)(2,1)}, bf16[2,2,2,128,128]{4,3,2,1,0:T(8,128)(2,1)}, u32[]{:S(2)}, u32[]{:S(2)}) collective-permute-start(bf16[2,2,2,128,128]{4,3,2,1,0:T(8,128)(2,1)} %cornered.2), channel_id=1, source_target_pairs={{1,2},{2,1},{5,6},{6,5},{9,10},{10,9},{13,14},{14,13},{17,18},{18,... | collective-permute-start | bytes 786440 | tf_op jit(solution)/shard_map/ppermute | solution.py:27
  4.4 46.2 %collective-permute-start.1 = (bf16[2,1,2,512,512]{4,3,2,1,0:T(8,128)(2,1)}, bf16[2,1,2,512,512]{4,3,2,1,0:T(8,128)(2,1)}, u32[]{:S(2)}, u32[]{:S(2)}) collective-permute-start(bf16[2,1,2,512,512]{4,3,2,1,0:T(8,128)(2,1)} %own.2), channel_id=1, source_target_pairs={{0,4},{2,6},{4,8},{5,1},{6,10},{7,3},{8,12},{9,5},{10,14},{11,7},{... | collective-permute-start | bytes 6291464 | tf_op jit(solution)/shard_map/ppermute | solution.py:17
  9.3 55.0 %collective-permute-start.2 = (bf16[2,1,2,512,512]{4,3,2,1,0:T(8,128)(2,1)}, bf16[2,1,2,512,512]{4,3,2,1,0:T(8,128)(2,1)}, u32[]{:S(2)}, u32[]{:S(2)}) collective-permute-start(bf16[2,1,2,512,512]{4,3,2,1,0:T(8,128)(2,1)} %own.2), channel_id=1, source_target_pairs={{1,5},{3,7},{4,0},{5,9},{6,2},{7,11},{8,4},{9,13},{10,6},{11,15},{... | collective-permute-start | bytes 6291464 | tf_op jit(solution)/shard_map/ppermute | solution.py:17
  20.2 10.2 %copy-start = (bf16[2,1,2,512,512]{4,3,2,1,0:T(8,128)(2,1)S(1)}, bf16[2,1,2,512,512]{4,3,2,1,0:T(8,128)(2,1)}, u32[]{:S(2)}) copy-start(bf16[2,1,2,512,512]{4,3,2,1,0:T(8,128)(2,1)} %own.3) | copy-start | bytes 6291460
  22.3 15.1 %collective-permute-start.3 = (bf16[2,2,2,128,128]{4,3,2,1,0:T(8,128)(2,1)}, bf16[2,2,2,128,128]{4,3,2,1,0:T(8,128)(2,1)S(1)}, u32[]{:S(2)}, u32[]{:S(2)}) collective-permute-start(bf16[2,2,2,128,128]{4,3,2,1,0:T(8,128)(2,1)} %cornered.3), channel_id=1, source_target_pairs={{0,1},{1,0},{2,3},{3,2},{4,5},{5,4},{6,7},{7,6},{8,9},{9,8},{10,11... | collective-permute-start | bytes 786440 | tf_op jit(solution)/shard_map/ppermute | solution.py:27
  31.5 47.5 %collective-permute-start.4 = (bf16[1,1,2,512,512]{4,3,2,1,0:T(8,128)(2,1)}, bf16[1,1,2,512,512]{4,3,2,1,0:T(8,128)(2,1)}, u32[]{:S(2)}, u32[]{:S(2)}) collective-permute-start(bf16[1,1,2,512,512]{4,3,2,1,0:T(8,128)(2,1)} %get-tuple-element.33), channel_id=1, source_target_pairs={{0,4},{2,6},{4,8},{5,1},{6,10},{7,3},{8,12},{9,5},{10,14},{11,7},{... | collective-permute-start | bytes 3145736 | tf_op jit(solution)/shard_map/ppermute | solution.py:17
  33.7 53.0 %collective-permute-start.5 = (bf16[1,1,2,512,512]{4,3,2,1,0:T(8,128)(2,1)S(1)}, bf16[1,1,2,512,512]{4,3,2,1,0:T(8,128)(2,1)}, u32[]{:S(2)}, u32[]{:S(2)}) collective-permute-start(bf16[1,1,2,512,512]{4,3,2,1,0:T(8,128)(2,1)S(1)} %get-tuple-element.32), channel_id=1, source_target_pairs={{1,5},{3,7},{4,0},{5,9},{6,2},{7,11},{8,4},{9,13},{10,6},{11,15},{... | collective-permute-start | bytes 3145736 | tf_op jit(solution)/shard_map/ppermute | solution.py:17
  37.4 29.0 %copy-start.1 = (bf16[2,2,2,128,128]{4,3,2,1,0:T(8,128)(2,1)}, bf16[2,2,2,128,128]{4,3,2,1,0:T(8,128)(2,1)S(1)}, u32[]{:S(2)}) copy-start(bf16[2,2,2,128,128]{4,3,2,1,0:T(8,128)(2,1)S(1)} %collective-permute-done.3.inner) | copy-start | bytes 786436
  37.4 61.4 %collective-permute-start.6 = (bf16[2,512,512]{2,1,0:T(8,128)(2,1)}, bf16[2,512,512]{2,1,0:T(8,128)(2,1)S(1)}, u32[]{:S(2)}, u32[]{:S(2)}) collective-permute-start(bf16[2,512,512]{2,1,0:T(8,128)(2,1)} %get-tuple-element.30), channel_id=1, source_target_pairs={{0,4},{2,6},{4,8},{5,1},{6,10},{7,3},{8,12},{9,5},{10,14},{11,7},{... | collective-permute-start | bytes 3145736 | tf_op jit(solution)/shard_map/ppermute | solution.py:17
  64.3 41.9 %collective-permute-start.7 = (bf16[2,512,512]{2,1,0:T(8,128)(2,1)}, bf16[2,512,512]{2,1,0:T(8,128)(2,1)S(1)}, u32[]{:S(2)}, u32[]{:S(2)}) collective-permute-start(bf16[2,512,512]{2,1,0:T(8,128)(2,1)} %get-tuple-element.31), channel_id=1, source_target_pairs={{1,5},{3,7},{4,0},{5,9},{6,2},{7,11},{8,4},{9,13},{10,6},{11,15},{... | collective-permute-start | bytes 3145736 | tf_op jit(solution)/shard_map/ppermute | solution.py:17
where the time goes:
time: 111 us; the launch traced here: 110 us
  Pallas kernels  38.2 us (34%)
  waiting for transfers between devices  35.5 us (32%)
  starting transfers between devices  30.6 us (28%)
  other arithmetic  3.96 us (4%)
  local copies, waits for them, and re-layouts  1.11 us (1%)
    pallas_call x6, Pallas kernels, call(): pl.pallas_call(kernel, grid_spec=pltpu.PrefetchScalarGridSpec(num_scalar_...  38.2 us
    ppermute x6, waiting for transfers between devices, shifted(): return lax.ppermute(x, ('energy', 'cuts'), pairs)  35.5 us
    ppermute x6, starting transfers between devices, shifted(): return lax.ppermute(x, ('energy', 'cuts'), pairs)  21.1 us
    ppermute x2, starting transfers between devices, swapped(): return lax.ppermute(x, ('energy', 'cuts'), pairs)  9.52 us
    convert_element_type x1, other arithmetic, added(): (near.astype(jnp.float32) + far.astype(jnp.float32)).astype(jnp.bfloat16)  3.95 us
  transfers between devices with their start and end apart: 8, of which 4 were waited for; matrix products, arithmetic and copies ran while one was open for 1% of the time, Pallas kernels for 33%

commit v1 on v0

--- a/solution.py
+++ b/solution.py
@@ -54,52 +54,43 @@
     )(*scalars, *operands)
 
 
-def corner_kernel(inside, low_top, high_top, low_bottom, high_bottom, out):
-    core = lax.axis_index("cuts") & 1
-    for kind, (top, bottom) in enumerate(((low_top, low_bottom), (high_top, high_bottom))):
-        upper = core == 1 if inside else core == 0
-        out[:, kind] = jnp.where(upper, top[:, 0], bottom[:, 0])
+def corner_kernel(inside, width, lesser, greater, out, place, sems):
+    cut = lax.axis_index("cuts")
+    core = cut & 1
+    last = (lesser.shape[-1] - width) // width
+    upper = (1 - core if inside else core) * last
+    edge = pl.ds(pl.multiple_of(upper * width, width), width)
+    copies = [
+        pltpu.make_async_copy(green.at[:, 0, :, edge, edge], out.at[:, kind], sems.at[kind])
+        for kind, green in enumerate((lesser, greater))
+    ]
+    for copy in copies:
+        copy.start()
+    place[0] = cut
+    place[1] = core
+    for copy in copies:
+        copy.wait()
 
 
 def cornered(inside, width, lesser, greater):
     parts = lesser.shape[2]
-    last = lesser.shape[-1] // width - 1
     shape = (2, 2, parts, width, width)
-    block = (2, 1, parts, width, width)
-    top = pl.BlockSpec(block, lambda i: (0, 0, 0, 0, 0))
-    bottom = pl.BlockSpec(block, lambda i: (0, 0, 0, last, last))
-    return call(
-        lambda *refs: corner_kernel(inside, *refs),
+    anywhere = pl.BlockSpec(memory_space=pl.ANY)
+    return call(
+        lambda *refs: corner_kernel(inside, width, *refs),
         "cornered",
         (),
-        (lesser, greater, lesser, greater),
+        (lesser, greater),
         (1,),
-        [top, top, bottom, bottom],
-        pl.BlockSpec(shape, lambda i: (0, 0, 0, 0, 0)),
-        jax.ShapeDtypeStruct(shape, lesser.dtype),
+        [anywhere, anywhere],
+        [
+            pl.BlockSpec(shape, lambda i: (0, 0, 0, 0, 0)),
+            pl.BlockSpec(memory_space=pltpu.SMEM),
+        ],
+        [jax.ShapeDtypeStruct(shape, lesser.dtype), jax.ShapeDtypeStruct((2,), jnp.int32)],
         60,
         0,
-    )
-
-
-def place_kernel(out):
-    cut = lax.axis_index("cuts")
-    out[0] = cut
-    out[1] = cut & 1
-
-
-def placed():
-    return call(
-        place_kernel,
-        "placed",
-        (),
-        (),
-        (),
-        [],
-        pl.BlockSpec(memory_space=pltpu.SMEM),
-        jax.ShapeDtypeStruct((2,), jnp.int32),
-        60,
-        10**12,
+        scratch=[pltpu.SemaphoreType.DMA((2,))],
     )
 
 
@@ -329,10 +320,32 @@
     )
 
 
-def added(core, near, first, second):
-    energy = lax.broadcasted_iota(jnp.int32, near.shape, 0)
-    far = jnp.where(energy == core, first[None, None], second[None, None])
-    return (near.astype(jnp.float32) + far.astype(jnp.float32)).astype(jnp.bfloat16)
+def add_kernel(place, near, far, out):
+    mixed = near[0, 0, 0].astype(jnp.float32) + far[0].astype(jnp.float32)
+    out[0, 0, 0] = mixed.astype(out.dtype)
+
+
+def added(slot, place, near, far):
+    parts, orbitals = far.shape[0], far.shape[-1]
+    rows = orbitals // 2
+
+    def energy_at(p, r, place):
+        return (place[1] if slot == 0 else 1 - place[1], 0, p, r, 0)
+
+    block = pl.BlockSpec((1, 1, 1, rows, orbitals), energy_at)
+    return call(
+        add_kernel,
+        "added",
+        (place,),
+        (near, far),
+        (parts, orbitals // rows),
+        [block, pl.BlockSpec((1, rows, orbitals), lambda p, r, *_: (p, r, 0))],
+        block,
+        jax.ShapeDtypeStruct(near.shape, near.dtype),
+        48,
+        orbitals**2,
+        input_output_aliases={1: 0},
+    )
 
 
 def body(lesser, greater, couplings, rim_couple, bose_factor, offsets, pattern):
@@ -341,8 +354,9 @@
     width = rim_couple.shape[-1]
     core = lax.axis_index("cuts") & 1
 
-    outer = swapped(cornered(False, width, lesser, greater), energies, cuts, False)
-    place, lesser_sent = lax.optimization_barrier((placed(), lesser))
+    outer, place = cornered(False, width, lesser, greater)
+    outer = swapped(outer, energies, cuts, False)
+    place, lesser_sent = lax.optimization_barrier((place, lesser))
     low = [shifted(lesser_sent, energies, cuts, first) for first in (True, False)]
     near = [lax.dynamic_slice_in_dim(greater, at, 1, 0) for at in (1 - core, core)]
     outer, place = lax.optimization_barrier((outer, place))
@@ -351,7 +365,7 @@
 
     first, second = far_terms(scalars, bose_factor, greater, couplings)
     second, lesser_corner = lax.optimization_barrier((second, lesser))
-    inner = swapped(cornered(True, width, lesser_corner, greater), energies, cuts, True)
+    inner = swapped(cornered(True, width, lesser_corner, greater)[0], energies, cuts, True)
     inner, first = lax.optimization_barrier((inner, first))
     corners = (inner, outer)
     first = shifted(first, energies, cuts, True)
@@ -364,7 +378,7 @@
     kept = greater_terms(
         scalars, bose_factor, greater, *high, corners, low_kept, couplings, rim_couple
     )
-    return low_out, added(core, kept, first, second)
+    return low_out, added(1, place, added(0, place, kept, first), second)
 
 
 def solution(mesh):

time: 111 us -> 176 us (1.59)
  the two profiles are of different devices: /device:TPU:110 before, /device:TPU:144 now
where the time goes in v1:
time: 176 us; the launch traced here: 175 us
  waiting for transfers between devices  90.4 us (51%)
  Pallas kernels  50.6 us (29%)
  starting transfers between devices  32.4 us (18%)
    ppermute x2, waiting for transfers between devices, swapped(): return lax.ppermute(x, ('energy', 'cuts'), pairs)  87.3 us
    pallas_call x7, Pallas kernels, call(): pl.pallas_call(kernel, grid_spec=pltpu.PrefetchScalarGridSpec(num_scalar_...  50.6 us
    ppermute x6, starting transfers between devices, shifted(): return lax.ppermute(x, ('energy', 'cuts'), pairs)  30.4 us
  transfers between devices with their start and end apart: 8, of which 2 were waited for; matrix products, arithmetic and copies ran while one was open for 1% of the time, Pallas kernels for 26%

profile of v1, /device:TPU:144, one launch (start us, length us, event | category | flops | bytes accessed | tf_op | source)
XLA Modules:
  0.0 175.4 jit_solution(15936141642065825882)
XLA Ops:
  0.6 1.7 cornered.2
  2.4 1.9 %collective-permute-start = (bf16[2,2,2,128,128]{4,3,2,1,0:T(8,128)(2,1)}, bf16[2,2,2,128,128]{4,3,2,1,0:T(8,128)(2,1)S(1)}, u32[]{:S(2)}, u32[]{:S(2)}) collective-permute-start(bf16[2,2,2,128,128]{4,3,2,1,0:T(8,128)(2,1)} %get-tuple-element.20), channel_id=1, source_target_pairs={{1,2},{2,1},{5,6},{6,5},{9,10},{10,9},{13,14},{14,13},{17,18},{18,... | collective-permute-start | bytes 786440 | tf_op jit(solution)/shard_map/ppermute | solution.py:27
  4.3 3.4 %collective-permute-start.1 = (bf16[2,1,2,512,512]{4,3,2,1,0:T(8,128)(2,1)}, bf16[2,1,2,512,512]{4,3,2,1,0:T(8,128)(2,1)}, u32[]{:S(2)}, u32[]{:S(2)}) collective-permute-start(bf16[2,1,2,512,512]{4,3,2,1,0:T(8,128)(2,1)} %own.2), channel_id=1, source_target_pairs={{0,4},{2,6},{4,8},{5,1},{6,10},{7,3},{8,12},{9,5},{10,14},{11,7},{... | collective-permute-start | bytes 6291464 | tf_op jit(solution)/shard_map/ppermute | solution.py:17
  7.7 6.7 %collective-permute-start.2 = (bf16[2,1,2,512,512]{4,3,2,1,0:T(8,128)(2,1)}, bf16[2,1,2,512,512]{4,3,2,1,0:T(8,128)(2,1)}, u32[]{:S(2)}, u32[]{:S(2)}) collective-permute-start(bf16[2,1,2,512,512]{4,3,2,1,0:T(8,128)(2,1)} %own.2), channel_id=1, source_target_pairs={{1,5},{3,7},{4,0},{5,9},{6,2},{7,11},{8,4},{9,13},{10,6},{11,15},{... | collective-permute-start | bytes 6291464 | tf_op jit(solution)/shard_map/ppermute | solution.py:17
  14.4 87.3 %collective-permute-done.outer = bf16[2,2,2,128,128]{4,3,2,1,0:T(8,128)(2,1)S(1)} collective-permute-done((bf16[2,2,2,128,128]{4,3,2,1,0:T(8,128)(2,1)}, bf16[2,2,2,128,128]{4,3,2,1,0:T(8,128)(2,1)S(1)}, u32[]{:S(2)}, u32[]{:S(2)}) %collective-permute-start) | collective-permute-done | bytes 262176 | tf_op jit(solution)/shard_map/ppermute | solution.py:27
  101.6 0.0 copy-start.2
  101.6 9.0 %far_terms.1 = (bf16[2,512,512]{2,1,0:T(8,128)(2,1)}, bf16[2,512,512]{2,1,0:T(8,128)(2,1)}) custom-call(s32[2]{0:T(128)} %get-tuple-element.23.place, s32[3]{0:T(128)} %offsets.5, s32[4,3]{1,0:T(4,128)} %pattern.5, f32[3]{0:T(128)} %bose.5, bf16[2,1,2,512,512]{4,3,2,1,0:T(8,128)(2,1)} %own.3, bf16[1,3,512,512]{3,2,1,0:T(8,128)(2,1)} %couple.5), custom_call_target="tpu_custom_call" | custom-call | flops 25769803776 | bytes 4194304 | tf_op jit(solution)/shard_map/far_terms/pallas_call | solution.py:40
  110.6 0.0 copy-done.2
  110.6 0.0 copy-start.1
  110.6 1.9 %cornered.3 = (bf16[2,2,2,128,128]{4,3,2,1,0:T(8,128)(2,1)}, s32[2]{0:T(128)}) custom-call(bf16[2,1,2,512,512]{4,3,2,1,0:T(8,128)(2,1)} %own.2, bf16[2,1,2,512,512]{4,3,2,1,0:T(8,128)(2,1)} %own.3), custom_call_target="tpu_custom_call" | custom-call | bytes 4194304 | tf_op jit(solution)/shard_map/cornered/pallas_call | solution.py:40
  112.5 0.1 collective-permute-start.3
  112.6 0.0 copy-done.1
  112.6 1.2 constant_dynamic-slice_fusion
  113.8 1.9 %collective-permute-start.4 = (bf16[1,1,2,512,512]{4,3,2,1,0:T(8,128)(2,1)}, bf16[1,1,2,512,512]{4,3,2,1,0:T(8,128)(2,1)}, u32[]{:S(2)}, u32[]{:S(2)}) collective-permute-start(bf16[1,1,2,512,512]{4,3,2,1,0:T(8,128)(2,1)} %get-tuple-element.39), channel_id=1, source_target_pairs={{0,4},{2,6},{4,8},{5,1},{6,10},{7,3},{8,12},{9,5},{10,14},{11,7},{... | collective-permute-start | bytes 3145736 | tf_op jit(solution)/shard_map/ppermute | solution.py:17
  115.7 8.1 %collective-permute-start.5 = (bf16[1,1,2,512,512]{4,3,2,1,0:T(8,128)(2,1)S(1)}, bf16[1,1,2,512,512]{4,3,2,1,0:T(8,128)(2,1)}, u32[]{:S(2)}, u32[]{:S(2)}) collective-permute-start(bf16[1,1,2,512,512]{4,3,2,1,0:T(8,128)(2,1)S(1)} %get-tuple-element.38), channel_id=1, source_target_pairs={{1,5},{3,7},{4,0},{5,9},{6,2},{7,11},{8,4},{9,13},{10,6},{11,15},{... | collective-permute-start | bytes 3145736 | tf_op jit(solution)/shard_map/ppermute | solution.py:17
  123.8 0.0 collective-permute-done.3.inner
  123.9 0.0 copy-start.3
  123.9 1.9 %collective-permute-start.6 = (bf16[2,512,512]{2,1,0:T(8,128)(2,1)}, bf16[2,512,512]{2,1,0:T(8,128)(2,1)S(1)}, u32[]{:S(2)}, u32[]{:S(2)}) collective-permute-start(bf16[2,512,512]{2,1,0:T(8,128)(2,1)} %get-tuple-element.36), channel_id=1, source_target_pairs={{0,4},{2,6},{4,8},{5,1},{6,10},{7,3},{8,12},{9,5},{10,14},{11,7},{... | collective-permute-start | bytes 3145736 | tf_op jit(solution)/shard_map/ppermute | solution.py:17
  125.8 0.0 collective-permute-done.1.first
  125.8 0.0 collective-permute-done.2.second
  125.8 8.3 %collective-permute-start.7 = (bf16[2,512,512]{2,1,0:T(8,128)(2,1)}, bf16[2,512,512]{2,1,0:T(8,128)(2,1)S(1)}, u32[]{:S(2)}, u32[]{:S(2)}) collective-permute-start(bf16[2,512,512]{2,1,0:T(8,128)(2,1)} %get-tuple-element.37), channel_id=1, source_target_pairs={{1,5},{3,7},{4,0},{5,9},{6,2},{7,11},{8,4},{9,13},{10,6},{11,15},{... | collective-permute-start | bytes 3145736 | tf_op jit(solution)/shard_map/ppermute | solution.py:17
  134.1 0.0 copy-done.3
  134.1 15.3 %lesser_terms.1 = (bf16[2,1,2,512,512]{4,3,2,1,0:T(8,128)(2,1)}, f32[2,2,512,512]{3,2,1,0:T(8,128)}) custom-call(s32[2]{0:T(128)} %get-tuple-element.23.place, s32[3]{0:T(128)} %offsets.5, s32[4,3]{1,0:T(4,128)} %pattern.5, f32[3]{0:T(128)} %bose.5, bf16[2,1,2,512,512]{4,3,2,1,0:T(8,128)(2,1)} %own.2, ...), custom_call_target="tpu_custom_call" | custom-call | flops 12884901888 | bytes 4194304 | tf_op jit(solution)/shard_map/lesser_terms/pallas_call | solution.py:40
  149.5 0.0 collective-permute-done.4.first
  149.5 0.0 collective-permute-done.5.second
  149.5 0.0 copy-start
  149.5 14.7 %greater_terms.1.near = bf16[2,1,2,512,512]{4,3,2,1,0:T(8,128)(2,1)} custom-call(s32[2]{0:T(128)} %get-tuple-element.23.place, s32[3]{0:T(128)} %offsets.5, s32[4,3]{1,0:T(4,128)} %pattern.5, f32[3]{0:T(128)} %bose.5, bf16[2,1,2,512,512]{4,3,2,1,0:T(8,128)(2,1)} %own.3, bf16[1,1,2,512,512]{4,3,2,1,0:T(8,128)(2,1)} %collective-permute-done.4.first, ...), custom_call_target="tpu_custom_call" | custom-call | flops 12884901888 | bytes 4194304 | tf_op jit(solution)/shard_map/greater_terms/pallas_call | solution.py:40
  164.2 3.1 %collective-permute-done.6.far = bf16[2,512,512]{2,1,0:T(8,128)(2,1)S(1)} collective-permute-done((bf16[2,512,512]{2,1,0:T(8,128)(2,1)}, bf16[2,512,512]{2,1,0:T(8,128)(2,1)S(1)}, u32[]{:S(2)}, u32[]{:S(2)}) %collective-permute-start.6) | collective-permute-done | bytes 1048608 | tf_op jit(solution)/shard_map/ppermute | solution.py:17
  167.3 0.0 copy-done
  167.3 4.0 %added.2.near = bf16[2,1,2,512,512]{4,3,2,1,0:T(8,128)(2,1)} custom-call(s32[2]{0:T(128)S(1)} %copy-done, bf16[2,1,2,512,512]{4,3,2,1,0:T(8,128)(2,1)} %greater_terms.1.near, bf16[2,512,512]{2,1,0:T(8,128)(2,1)S(1)} %collective-permute-done.6.far), custom_call_target="tpu_custom_call", output_to_operand_aliasing={{}: (1, {})} | custom-call | flops 262144 | bytes 4194304 | tf_op jit(solution)/shard_map/added/pallas_call | solution.py:40
  171.3 0.0 collective-permute-done.7.far
  171.3 4.0 %added.3 = bf16[2,1,2,512,512]{4,3,2,1,0:T(8,128)(2,1)} custom-call(s32[2]{0:T(128)S(1)} %copy-done, bf16[2,1,2,512,512]{4,3,2,1,0:T(8,128)(2,1)} %added.2.near, bf16[2,512,512]{2,1,0:T(8,128)(2,1)S(1)} %collective-permute-done.7.far), custom_call_target="tpu_custom_call", output_to_operand_aliasing={{}: (1, {})} | custom-call | flops 262144 | bytes 4194304 | tf_op jit(solution)/shard_map/added/pallas_call | solution.py:40
Async XLA Ops:
  2.4 99.3 %collective-permute-start = (bf16[2,2,2,128,128]{4,3,2,1,0:T(8,128)(2,1)}, bf16[2,2,2,128,128]{4,3,2,1,0:T(8,128)(2,1)S(1)}, u32[]{:S(2)}, u32[]{:S(2)}) collective-permute-start(bf16[2,2,2,128,128]{4,3,2,1,0:T(8,128)(2,1)} %get-tuple-element.20), channel_id=1, source_target_pairs={{1,2},{2,1},{5,6},{6,5},{9,10},{10,9},{13,14},{14,13},{17,18},{18,... | collective-permute-start | bytes 786440 | tf_op jit(solution)/shard_map/ppermute | solution.py:27
  4.3 121.5 %collective-permute-start.1 = (bf16[2,1,2,512,512]{4,3,2,1,0:T(8,128)(2,1)}, bf16[2,1,2,512,512]{4,3,2,1,0:T(8,128)(2,1)}, u32[]{:S(2)}, u32[]{:S(2)}) collective-permute-start(bf16[2,1,2,512,512]{4,3,2,1,0:T(8,128)(2,1)} %own.2), channel_id=1, source_target_pairs={{0,4},{2,6},{4,8},{5,1},{6,10},{7,3},{8,12},{9,5},{10,14},{11,7},{... | collective-permute-start | bytes 6291464 | tf_op jit(solution)/shard_map/ppermute | solution.py:17
  7.7 118.1 %collective-permute-start.2 = (bf16[2,1,2,512,512]{4,3,2,1,0:T(8,128)(2,1)}, bf16[2,1,2,512,512]{4,3,2,1,0:T(8,128)(2,1)}, u32[]{:S(2)}, u32[]{:S(2)}) collective-permute-start(bf16[2,1,2,512,512]{4,3,2,1,0:T(8,128)(2,1)} %own.2), channel_id=1, source_target_pairs={{1,5},{3,7},{4,0},{5,9},{6,2},{7,11},{8,4},{9,13},{10,6},{11,15},{... | collective-permute-start | bytes 6291464 | tf_op jit(solution)/shard_map/ppermute | solution.py:17
  101.6 9.0 %copy-start.2 = (bf16[2,2,2,128,128]{4,3,2,1,0:T(8,128)(2,1)}, bf16[2,2,2,128,128]{4,3,2,1,0:T(8,128)(2,1)S(1)}, u32[]{:S(2)}) copy-start(bf16[2,2,2,128,128]{4,3,2,1,0:T(8,128)(2,1)S(1)} %collective-permute-done.outer) | copy-start | bytes 786436
  110.6 2.0 %copy-start.1 = (bf16[2,1,2,512,512]{4,3,2,1,0:T(8,128)(2,1)S(1)}, bf16[2,1,2,512,512]{4,3,2,1,0:T(8,128)(2,1)}, u32[]{:S(2)}) copy-start(bf16[2,1,2,512,512]{4,3,2,1,0:T(8,128)(2,1)} %own.3) | copy-start | bytes 6291460
  112.5 11.4 %collective-permute-start.3 = (bf16[2,2,2,128,128]{4,3,2,1,0:T(8,128)(2,1)}, bf16[2,2,2,128,128]{4,3,2,1,0:T(8,128)(2,1)S(1)}, u32[]{:S(2)}, u32[]{:S(2)}) collective-permute-start(bf16[2,2,2,128,128]{4,3,2,1,0:T(8,128)(2,1)} %get-tuple-element.30), channel_id=1, source_target_pairs={{0,1},{1,0},{2,3},{3,2},{4,5},{5,4},{6,7},{7,6},{8,9},{9,8},{10,11... | collective-permute-start | bytes 786440 | tf_op jit(solution)/shard_map/ppermute | solution.py:27
  113.8 35.7 %collective-permute-start.4 = (bf16[1,1,2,512,512]{4,3,2,1,0:T(8,128)(2,1)}, bf16[1,1,2,512,512]{4,3,2,1,0:T(8,128)(2,1)}, u32[]{:S(2)}, u32[]{:S(2)}) collective-permute-start(bf16[1,1,2,512,512]{4,3,2,1,0:T(8,128)(2,1)} %get-tuple-element.39), channel_id=1, source_target_pairs={{0,4},{2,6},{4,8},{5,1},{6,10},{7,3},{8,12},{9,5},{10,14},{11,7},{... | collective-permute-start | bytes 3145736 | tf_op jit(solution)/shard_map/ppermute | solution.py:17
  115.7 33.8 %collective-permute-start.5 = (bf16[1,1,2,512,512]{4,3,2,1,0:T(8,128)(2,1)S(1)}, bf16[1,1,2,512,512]{4,3,2,1,0:T(8,128)(2,1)}, u32[]{:S(2)}, u32[]{:S(2)}) collective-permute-start(bf16[1,1,2,512,512]{4,3,2,1,0:T(8,128)(2,1)S(1)} %get-tuple-element.38), channel_id=1, source_target_pairs={{1,5},{3,7},{4,0},{5,9},{6,2},{7,11},{8,4},{9,13},{10,6},{11,15},{... | collective-permute-start | bytes 3145736 | tf_op jit(solution)/shard_map/ppermute | solution.py:17
  123.9 10.3 %copy-start.3 = (bf16[2,2,2,128,128]{4,3,2,1,0:T(8,128)(2,1)}, bf16[2,2,2,128,128]{4,3,2,1,0:T(8,128)(2,1)S(1)}, u32[]{:S(2)}) copy-start(bf16[2,2,2,128,128]{4,3,2,1,0:T(8,128)(2,1)S(1)} %collective-permute-done.3.inner) | copy-start | bytes 786436
  123.9 43.5 %collective-permute-start.6 = (bf16[2,512,512]{2,1,0:T(8,128)(2,1)}, bf16[2,512,512]{2,1,0:T(8,128)(2,1)S(1)}, u32[]{:S(2)}, u32[]{:S(2)}) collective-permute-start(bf16[2,512,512]{2,1,0:T(8,128)(2,1)} %get-tuple-element.36), channel_id=1, source_target_pairs={{0,4},{2,6},{4,8},{5,1},{6,10},{7,3},{8,12},{9,5},{10,14},{11,7},{... | collective-permute-start | bytes 3145736 | tf_op jit(solution)/shard_map/ppermute | solution.py:17
  125.8 45.5 %collective-permute-start.7 = (bf16[2,512,512]{2,1,0:T(8,128)(2,1)}, bf16[2,512,512]{2,1,0:T(8,128)(2,1)S(1)}, u32[]{:S(2)}, u32[]{:S(2)}) collective-permute-start(bf16[2,512,512]{2,1,0:T(8,128)(2,1)} %get-tuple-element.37), channel_id=1, source_target_pairs={{1,5},{3,7},{4,0},{5,9},{6,2},{7,11},{8,4},{9,13},{10,6},{11,15},{... | collective-permute-start | bytes 3145736 | tf_op jit(solution)/shard_map/ppermute | solution.py:17
  149.5 17.9 %copy-start = (s32[2]{0:T(128)S(1)}, s32[2]{0:T(128)}, u32[]{:S(2)}) copy-start(s32[2]{0:T(128)} %get-tuple-element.23.place) | copy-start | bytes 28

commit v2 on v0

--- a/solution.py
+++ b/solution.py
@@ -329,10 +329,10 @@
     )
 
 
-def added(core, near, first, second):
-    energy = lax.broadcasted_iota(jnp.int32, near.shape, 0)
-    far = jnp.where(energy == core, first[None, None], second[None, None])
-    return (near.astype(jnp.float32) + far.astype(jnp.float32)).astype(jnp.bfloat16)
+def added(near, at, far):
+    slab = lax.dynamic_index_in_dim(near, at, 0, keepdims=True)
+    slab = (slab.astype(jnp.float32) + far[None, None].astype(jnp.float32)).astype(near.dtype)
+    return lax.dynamic_update_slice_in_dim(near, slab, at, 0)
 
 
 def body(lesser, greater, couplings, rim_couple, bose_factor, offsets, pattern):
@@ -364,7 +364,7 @@
     kept = greater_terms(
         scalars, bose_factor, greater, *high, corners, low_kept, couplings, rim_couple
     )
-    return low_out, added(core, kept, first, second)
+    return low_out, added(added(kept, core, first), 1 - core, second)
 
 
 def solution(mesh):

time: 111 us -> 110 us (level)
  Pallas kernels: 38.2 us -> 35.8 us
  starting transfers between devices: 30.6 us -> 28.4 us
  waiting for transfers between devices: 35.5 us -> 37.6 us
    dynamic_update_slice x0 -> x2, other arithmetic: none -> 4.97 us  [added(): return lax.dynamic_update_slice_in_dim(near, slab, at, 0)]
    ppermute x2, starting transfers between devices: 9.52 us -> 4.65 us  [swapped(): return lax.ppermute(x, ('energy', 'cuts'), pairs)]
    convert_element_type x1 -> x0, other arithmetic: 3.95 us -> none  [added(): (near.astype(jnp.float32) + far.astype(jnp.float32)).astype(jnp.bfloat16)]
    ppermute x6, starting transfers between devices: 21.1 us -> 23.8 us  [shifted(): return lax.ppermute(x, ('energy', 'cuts'), pairs)]
    pallas_call x6, Pallas kernels: 38.2 us -> 35.8 us  [call(): pl.pallas_call(kernel, grid_spec=pltpu.PrefetchScalarGridSpec(num_scalar_...]
    ppermute x6, waiting for transfers between devices: 35.5 us -> 37.5 us  [shifted(): return lax.ppermute(x, ('energy', 'cuts'), pairs)]
  transfers between devices with their start and end apart: 8 -> 8, of which waited for: 4 -> 4; matrix products, arithmetic and copies ran while one was open for 1% -> 3% of each run, Pallas kernels for 33% -> 31%
where the time goes in v2:
time: 110 us; the launch traced here: 109 us
  waiting for transfers between devices  37.6 us (34%)
  Pallas kernels  35.8 us (33%)
  starting transfers between devices  28.4 us (26%)
  other arithmetic  4.97 us (5%)
  local copies, waits for them, and re-layouts  1.18 us (1%)
    ppermute x6, waiting for transfers between devices, shifted(): return lax.ppermute(x, ('energy', 'cuts'), pairs)  37.5 us
    pallas_call x6, Pallas kernels, call(): pl.pallas_call(kernel, grid_spec=pltpu.PrefetchScalarGridSpec(num_scalar_...  35.8 us
    ppermute x6, starting transfers between devices, shifted(): return lax.ppermute(x, ('energy', 'cuts'), pairs)  23.8 us
    dynamic_update_slice x2, other arithmetic, added(): return lax.dynamic_update_slice_in_dim(near, slab, at, 0)  4.97 us
    ppermute x2, starting transfers between devices, swapped(): return lax.ppermute(x, ('energy', 'cuts'), pairs)  4.65 us
  transfers between devices with their start and end apart: 8, of which 4 were waited for; matrix products, arithmetic and copies ran while one was open for 3% of the time, Pallas kernels for 31%

profile of v2, /device:TPU:110, one launch (start us, length us, event | category | flops | bytes accessed | tf_op | source)
XLA Modules:
  0.0 108.7 jit_solution(12950356429416190494)
XLA Ops:
  0.6 1.9 %cornered.2 = bf16[2,2,2,128,128]{4,3,2,1,0:T(8,128)(2,1)} custom-call(bf16[2,1,2,512,512]{4,3,2,1,0:T(8,128)(2,1)} %own.2, bf16[2,1,2,512,512]{4,3,2,1,0:T(8,128)(2,1)} %own.3, bf16[2,1,2,512,512]{4,3,2,1,0:T(8,128)(2,1)} %own.2, bf16[2,1,2,512,512]{4,3,2,1,0:T(8,128)(2,1)} %own.3), custom_call_target="tpu_custom_call" | custom-call | bytes 4194304 | tf_op jit(solution)/shard_map/cornered/pallas_call | solution.py:40
  2.5 1.4 %collective-permute-start = (bf16[2,2,2,128,128]{4,3,2,1,0:T(8,128)(2,1)}, bf16[2,2,2,128,128]{4,3,2,1,0:T(8,128)(2,1)}, u32[]{:S(2)}, u32[]{:S(2)}) collective-permute-start(bf16[2,2,2,128,128]{4,3,2,1,0:T(8,128)(2,1)} %cornered.2), channel_id=1, source_target_pairs={{1,2},{2,1},{5,6},{6,5},{9,10},{10,9},{13,14},{14,13},{17,18},{18,... | collective-permute-start | bytes 786440 | tf_op jit(solution)/shard_map/ppermute | solution.py:27
  3.9 0.5 placed.1.place
  4.4 4.8 %collective-permute-start.1 = (bf16[2,1,2,512,512]{4,3,2,1,0:T(8,128)(2,1)}, bf16[2,1,2,512,512]{4,3,2,1,0:T(8,128)(2,1)}, u32[]{:S(2)}, u32[]{:S(2)}) collective-permute-start(bf16[2,1,2,512,512]{4,3,2,1,0:T(8,128)(2,1)} %own.2), channel_id=1, source_target_pairs={{0,4},{2,6},{4,8},{5,1},{6,10},{7,3},{8,12},{9,5},{10,14},{11,7},{... | collective-permute-start | bytes 6291464 | tf_op jit(solution)/shard_map/ppermute | solution.py:17
  9.3 1.9 %collective-permute-start.2 = (bf16[2,1,2,512,512]{4,3,2,1,0:T(8,128)(2,1)}, bf16[2,1,2,512,512]{4,3,2,1,0:T(8,128)(2,1)}, u32[]{:S(2)}, u32[]{:S(2)}) collective-permute-start(bf16[2,1,2,512,512]{4,3,2,1,0:T(8,128)(2,1)} %own.2), channel_id=1, source_target_pairs={{1,5},{3,7},{4,0},{5,9},{6,2},{7,11},{8,4},{9,13},{10,6},{11,15},{... | collective-permute-start | bytes 6291464 | tf_op jit(solution)/shard_map/ppermute | solution.py:17
  11.2 0.0 collective-permute-done.outer
  11.2 6.5 %far_terms.1 = (bf16[2,512,512]{2,1,0:T(8,128)(2,1)}, bf16[2,512,512]{2,1,0:T(8,128)(2,1)}) custom-call(s32[2]{0:T(128)} %placed.1.place, s32[3]{0:T(128)} %offsets.5, s32[4,3]{1,0:T(4,128)} %pattern.5, f32[3]{0:T(128)} %bose.5, bf16[2,1,2,512,512]{4,3,2,1,0:T(8,128)(2,1)} %own.3, bf16[1,3,512,512]{3,2,1,0:T(8,128)(2,1)} %couple.5), custom_call_target="tpu_custom_call" | custom-call | flops 25769803776 | bytes 4194304 | tf_op jit(solution)/shard_map/far_terms/pallas_call | solution.py:40
  17.7 0.0 copy-start
  17.7 2.0 %cornered.3 = bf16[2,2,2,128,128]{4,3,2,1,0:T(8,128)(2,1)} custom-call(bf16[2,1,2,512,512]{4,3,2,1,0:T(8,128)(2,1)} %own.2, bf16[2,1,2,512,512]{4,3,2,1,0:T(8,128)(2,1)} %own.3, bf16[2,1,2,512,512]{4,3,2,1,0:T(8,128)(2,1)} %own.2, bf16[2,1,2,512,512]{4,3,2,1,0:T(8,128)(2,1)} %own.3), custom_call_target="tpu_custom_call" | custom-call | bytes 4194304 | tf_op jit(solution)/shard_map/cornered/pallas_call | solution.py:40
  19.8 3.3 %collective-permute-start.3 = (bf16[2,2,2,128,128]{4,3,2,1,0:T(8,128)(2,1)}, bf16[2,2,2,128,128]{4,3,2,1,0:T(8,128)(2,1)S(1)}, u32[]{:S(2)}, u32[]{:S(2)}) collective-permute-start(bf16[2,2,2,128,128]{4,3,2,1,0:T(8,128)(2,1)} %cornered.3), channel_id=1, source_target_pairs={{0,1},{1,0},{2,3},{3,2},{4,5},{5,4},{6,7},{7,6},{8,9},{9,8},{10,11... | collective-permute-start | bytes 786440 | tf_op jit(solution)/shard_map/ppermute | solution.py:27
  23.0 0.0 copy-done
  23.0 1.2 %constant_dynamic-slice_fusion = (bf16[1,1,2,512,512]{4,3,2,1,0:T(8,128)(2,1)S(1)}, bf16[1,1,2,512,512]{4,3,2,1,0:T(8,128)(2,1)}) fusion(bf16[2,1,2,512,512]{4,3,2,1,0:T(8,128)(2,1)S(1)} %copy-done, s32[]{:T(128)S(6)} %select_n.12, s32[]{:T(128)S(6)} %select_n.11), kind=kLoop, calls=%fused_computation.6 | loop fusion | bytes 4194312 | tf_op jit(solution)/shard_map/dynamic_slice | solution.py:347
  24.2 4.8 %collective-permute-start.4 = (bf16[1,1,2,512,512]{4,3,2,1,0:T(8,128)(2,1)}, bf16[1,1,2,512,512]{4,3,2,1,0:T(8,128)(2,1)}, u32[]{:S(2)}, u32[]{:S(2)}) collective-permute-start(bf16[1,1,2,512,512]{4,3,2,1,0:T(8,128)(2,1)} %get-tuple-element.33), channel_id=1, source_target_pairs={{0,4},{2,6},{4,8},{5,1},{6,10},{7,3},{8,12},{9,5},{10,14},{11,7},{... | collective-permute-start | bytes 3145736 | tf_op jit(solution)/shard_map/ppermute | solution.py:17
  29.1 1.9 %collective-permute-start.5 = (bf16[1,1,2,512,512]{4,3,2,1,0:T(8,128)(2,1)S(1)}, bf16[1,1,2,512,512]{4,3,2,1,0:T(8,128)(2,1)}, u32[]{:S(2)}, u32[]{:S(2)}) collective-permute-start(bf16[1,1,2,512,512]{4,3,2,1,0:T(8,128)(2,1)S(1)} %get-tuple-element.32), channel_id=1, source_target_pairs={{1,5},{3,7},{4,0},{5,9},{6,2},{7,11},{8,4},{9,13},{10,6},{11,15},{... | collective-permute-start | bytes 3145736 | tf_op jit(solution)/shard_map/ppermute | solution.py:17
  31.0 0.0 collective-permute-done.3.inner
  31.0 0.0 copy-start.1
  31.0 8.1 %collective-permute-start.6 = (bf16[2,512,512]{2,1,0:T(8,128)(2,1)}, bf16[2,512,512]{2,1,0:T(8,128)(2,1)S(1)}, u32[]{:S(2)}, u32[]{:S(2)}) collective-permute-start(bf16[2,512,512]{2,1,0:T(8,128)(2,1)} %get-tuple-element.30), channel_id=1, source_target_pairs={{0,4},{2,6},{4,8},{5,1},{6,10},{7,3},{8,12},{9,5},{10,14},{11,7},{... | collective-permute-start | bytes 3145736 | tf_op jit(solution)/shard_map/ppermute | solution.py:17
  39.2 11.4 %collective-permute-done.1.first = bf16[2,1,2,512,512]{4,3,2,1,0:T(8,128)(2,1)} collective-permute-done((bf16[2,1,2,512,512]{4,3,2,1,0:T(8,128)(2,1)}, bf16[2,1,2,512,512]{4,3,2,1,0:T(8,128)(2,1)}, u32[]{:S(2)}, u32[]{:S(2)}) %collective-permute-start.1) | collective-permute-done | bytes 2097184 | tf_op jit(solution)/shard_map/ppermute | solution.py:17
  50.6 13.7 %collective-permute-done.2.second = bf16[2,1,2,512,512]{4,3,2,1,0:T(8,128)(2,1)} collective-permute-done((bf16[2,1,2,512,512]{4,3,2,1,0:T(8,128)(2,1)}, bf16[2,1,2,512,512]{4,3,2,1,0:T(8,128)(2,1)}, u32[]{:S(2)}, u32[]{:S(2)}) %collective-permute-start.2) | collective-permute-done | bytes 2097184 | tf_op jit(solution)/shard_map/ppermute | solution.py:17
  64.3 2.1 %collective-permute-start.7 = (bf16[2,512,512]{2,1,0:T(8,128)(2,1)}, bf16[2,512,512]{2,1,0:T(8,128)(2,1)S(1)}, u32[]{:S(2)}, u32[]{:S(2)}) collective-permute-start(bf16[2,512,512]{2,1,0:T(8,128)(2,1)} %get-tuple-element.31), channel_id=1, source_target_pairs={{1,5},{3,7},{4,0},{5,9},{6,2},{7,11},{8,4},{9,13},{10,6},{11,15},{... | collective-permute-start | bytes 3145736 | tf_op jit(solution)/shard_map/ppermute | solution.py:17
  66.4 0.0 copy-done.1
  66.4 12.6 %lesser_terms.1 = (bf16[2,1,2,512,512]{4,3,2,1,0:T(8,128)(2,1)}, f32[2,2,512,512]{3,2,1,0:T(8,128)}) custom-call(s32[2]{0:T(128)} %placed.1.place, s32[3]{0:T(128)} %offsets.5, s32[4,3]{1,0:T(4,128)} %pattern.5, f32[3]{0:T(128)} %bose.5, bf16[2,1,2,512,512]{4,3,2,1,0:T(8,128)(2,1)} %own.2, bf16[2,1,2,512,512]{4,3,2,1,0:T(8,128)(2,1)} %collective-permute-done.1.first, ...), custom_call_target="tpu_custom_call" | custom-call | flops 12884901888 | bytes 4194304 | tf_op jit(solution)/shard_map/lesser_terms/pallas_call | solution.py:40
  79.0 0.0 collective-permute-done.4.first
  79.0 7.7 %collective-permute-done.5.second = bf16[1,1,2,512,512]{4,3,2,1,0:T(8,128)(2,1)} collective-permute-done((bf16[1,1,2,512,512]{4,3,2,1,0:T(8,128)(2,1)S(1)}, bf16[1,1,2,512,512]{4,3,2,1,0:T(8,128)(2,1)}, u32[]{:S(2)}, u32[]{:S(2)}) %collective-permute-start.5) | collective-permute-done | bytes 1048608 | tf_op jit(solution)/shard_map/ppermute | solution.py:17
  86.7 12.2 %greater_terms.1 = bf16[2,1,2,512,512]{4,3,2,1,0:T(8,128)(2,1)} custom-call(s32[2]{0:T(128)} %placed.1.place, s32[3]{0:T(128)} %offsets.5, s32[4,3]{1,0:T(4,128)} %pattern.5, f32[3]{0:T(128)} %bose.5, bf16[2,1,2,512,512]{4,3,2,1,0:T(8,128)(2,1)} %own.3, bf16[1,1,2,512,512]{4,3,2,1,0:T(8,128)(2,1)} %collective-permute-done.4.first, ...), custom_call_target="tpu_custom_call" | custom-call | flops 12884901888 | bytes 4194304 | tf_op jit(solution)/shard_map/greater_terms/pallas_call | solution.py:40
  99.0 0.0 collective-permute-done.6
  99.0 2.5 %fusion.2 = bf16[2,1,2,512,512]{4,3,2,1,0:T(8,128)(2,1)} fusion(bf16[2,1,2,512,512]{4,3,2,1,0:T(8,128)(2,1)} %greater_terms.1, s32[]{:T(128)S(6)} %select_n.12, bf16[2,512,512]{2,1,0:T(8,128)(2,1)S(1)} %collective-permute-done.6), kind=kLoop, calls=%fused_computation.4 | loop fusion | flops 2097152 | bytes 3145732 | tf_op jit(solution)/shard_map/dynamic_update_slice | solution.py:335
  101.5 4.7 %collective-permute-done.7 = bf16[2,512,512]{2,1,0:T(8,128)(2,1)S(1)} collective-permute-done((bf16[2,512,512]{2,1,0:T(8,128)(2,1)}, bf16[2,512,512]{2,1,0:T(8,128)(2,1)S(1)}, u32[]{:S(2)}, u32[]{:S(2)}) %collective-permute-start.7) | collective-permute-done | bytes 1048608 | tf_op jit(solution)/shard_map/ppermute | solution.py:17
  106.2 2.5 %fusion.3 = bf16[2,1,2,512,512]{4,3,2,1,0:T(8,128)(2,1)} fusion(bf16[2,1,2,512,512]{4,3,2,1,0:T(8,128)(2,1)} %fusion.2, s32[]{:T(128)S(6)} %select_n.11, bf16[2,512,512]{2,1,0:T(8,128)(2,1)S(1)} %collective-permute-done.7), kind=kLoop, calls=%fused_computation.5 | loop fusion | flops 2097152 | bytes 3145732 | tf_op jit(solution)/shard_map/dynamic_update_slice | solution.py:335
Async XLA Ops:
  2.5 8.7 %collective-permute-start = (bf16[2,2,2,128,128]{4,3,2,1,0:T(8,128)(2,1)}, bf16[2,2,2,128,128]{4,3,2,1,0:T(8,128)(2,1)}, u32[]{:S(2)}, u32[]{:S(2)}) collective-permute-start(bf16[2,2,2,128,128]{4,3,2,1,0:T(8,128)(2,1)} %cornered.2), channel_id=1, source_target_pairs={{1,2},{2,1},{5,6},{6,5},{9,10},{10,9},{13,14},{14,13},{17,18},{18,... | collective-permute-start | bytes 786440 | tf_op jit(solution)/shard_map/ppermute | solution.py:27
  4.4 46.2 %collective-permute-start.1 = (bf16[2,1,2,512,512]{4,3,2,1,0:T(8,128)(2,1)}, bf16[2,1,2,512,512]{4,3,2,1,0:T(8,128)(2,1)}, u32[]{:S(2)}, u32[]{:S(2)}) collective-permute-start(bf16[2,1,2,512,512]{4,3,2,1,0:T(8,128)(2,1)} %own.2), channel_id=1, source_target_pairs={{0,4},{2,6},{4,8},{5,1},{6,10},{7,3},{8,12},{9,5},{10,14},{11,7},{... | collective-permute-start | bytes 6291464 | tf_op jit(solution)/shard_map/ppermute | solution.py:17
  9.3 55.0 %collective-permute-start.2 = (bf16[2,1,2,512,512]{4,3,2,1,0:T(8,128)(2,1)}, bf16[2,1,2,512,512]{4,3,2,1,0:T(8,128)(2,1)}, u32[]{:S(2)}, u32[]{:S(2)}) collective-permute-start(bf16[2,1,2,512,512]{4,3,2,1,0:T(8,128)(2,1)} %own.2), channel_id=1, source_target_pairs={{1,5},{3,7},{4,0},{5,9},{6,2},{7,11},{8,4},{9,13},{10,6},{11,15},{... | collective-permute-start | bytes 6291464 | tf_op jit(solution)/shard_map/ppermute | solution.py:17
  17.7 5.3 %copy-start = (bf16[2,1,2,512,512]{4,3,2,1,0:T(8,128)(2,1)S(1)}, bf16[2,1,2,512,512]{4,3,2,1,0:T(8,128)(2,1)}, u32[]{:S(2)}) copy-start(bf16[2,1,2,512,512]{4,3,2,1,0:T(8,128)(2,1)} %own.3) | copy-start | bytes 6291460
  19.8 11.2 %collective-permute-start.3 = (bf16[2,2,2,128,128]{4,3,2,1,0:T(8,128)(2,1)}, bf16[2,2,2,128,128]{4,3,2,1,0:T(8,128)(2,1)S(1)}, u32[]{:S(2)}, u32[]{:S(2)}) collective-permute-start(bf16[2,2,2,128,128]{4,3,2,1,0:T(8,128)(2,1)} %cornered.3), channel_id=1, source_target_pairs={{0,1},{1,0},{2,3},{3,2},{4,5},{5,4},{6,7},{7,6},{8,9},{9,8},{10,11... | collective-permute-start | bytes 786440 | tf_op jit(solution)/shard_map/ppermute | solution.py:27
  24.2 54.8 %collective-permute-start.4 = (bf16[1,1,2,512,512]{4,3,2,1,0:T(8,128)(2,1)}, bf16[1,1,2,512,512]{4,3,2,1,0:T(8,128)(2,1)}, u32[]{:S(2)}, u32[]{:S(2)}) collective-permute-start(bf16[1,1,2,512,512]{4,3,2,1,0:T(8,128)(2,1)} %get-tuple-element.33), channel_id=1, source_target_pairs={{0,4},{2,6},{4,8},{5,1},{6,10},{7,3},{8,12},{9,5},{10,14},{11,7},{... | collective-permute-start | bytes 3145736 | tf_op jit(solution)/shard_map/ppermute | solution.py:17
  29.1 57.7 %collective-permute-start.5 = (bf16[1,1,2,512,512]{4,3,2,1,0:T(8,128)(2,1)S(1)}, bf16[1,1,2,512,512]{4,3,2,1,0:T(8,128)(2,1)}, u32[]{:S(2)}, u32[]{:S(2)}) collective-permute-start(bf16[1,1,2,512,512]{4,3,2,1,0:T(8,128)(2,1)S(1)} %get-tuple-element.32), channel_id=1, source_target_pairs={{1,5},{3,7},{4,0},{5,9},{6,2},{7,11},{8,4},{9,13},{10,6},{11,15},{... | collective-permute-start | bytes 3145736 | tf_op jit(solution)/shard_map/ppermute | solution.py:17
  31.0 35.4 %copy-start.1 = (bf16[2,2,2,128,128]{4,3,2,1,0:T(8,128)(2,1)}, bf16[2,2,2,128,128]{4,3,2,1,0:T(8,128)(2,1)S(1)}, u32[]{:S(2)}) copy-start(bf16[2,2,2,128,128]{4,3,2,1,0:T(8,128)(2,1)S(1)} %collective-permute-done.3.inner) | copy-start | bytes 786436
  31.0 67.9 %collective-permute-start.6 = (bf16[2,512,512]{2,1,0:T(8,128)(2,1)}, bf16[2,512,512]{2,1,0:T(8,128)(2,1)S(1)}, u32[]{:S(2)}, u32[]{:S(2)}) collective-permute-start(bf16[2,512,512]{2,1,0:T(8,128)(2,1)} %get-tuple-element.30), channel_id=1, source_target_pairs={{0,4},{2,6},{4,8},{5,1},{6,10},{7,3},{8,12},{9,5},{10,14},{11,7},{... | collective-permute-start | bytes 3145736 | tf_op jit(solution)/shard_map/ppermute | solution.py:17
  64.3 41.9 %collective-permute-start.7 = (bf16[2,512,512]{2,1,0:T(8,128)(2,1)}, bf16[2,512,512]{2,1,0:T(8,128)(2,1)S(1)}, u32[]{:S(2)}, u32[]{:S(2)}) collective-permute-start(bf16[2,512,512]{2,1,0:T(8,128)(2,1)} %get-tuple-element.31), channel_id=1, source_target_pairs={{1,5},{3,7},{4,0},{5,9},{6,2},{7,11},{8,4},{9,13},{10,6},{11,15},{... | collective-permute-start | bytes 3145736 | tf_op jit(solution)/shard_map/ppermute | solution.py:17

commit v3 on v2

--- a/solution.py
+++ b/solution.py
@@ -335,6 +335,49 @@
     return lax.dynamic_update_slice_in_dim(near, slab, at, 0)
 
 
+def last_kernel(place, near, far, partial, out, mixed, sems):
+    energy = 1 - place[1]
+    parts, orbitals = mixed.shape[0], mixed.shape[1]
+    rows = orbitals // 2
+    copies = []
+    for part in range(parts):
+        for half in range(2):
+            at = slice(half * rows, (half + 1) * rows)
+            value = near[part, at].astype(jnp.float32) + far[part, at].astype(jnp.float32)
+            mixed[part, at] = value.astype(mixed.dtype)
+            copy = pltpu.make_async_copy(
+                mixed.at[part, pl.ds(half * rows, rows)],
+                out.at[energy, 0, part, pl.ds(half * rows, rows)],
+                sems.at[part, half],
+            )
+            copy.start()
+            copies.append(copy)
+    for copy in copies:
+        copy.wait()
+
+
+def last_added(place, near, far, partial):
+    inside = pl.BlockSpec(memory_space=pltpu.VMEM)
+    anywhere = pl.BlockSpec(memory_space=pl.ANY)
+    return call(
+        last_kernel,
+        "last_added",
+        (place,),
+        (near, far, partial),
+        (),
+        [inside, inside, anywhere],
+        anywhere,
+        jax.ShapeDtypeStruct(partial.shape, partial.dtype),
+        48,
+        10**9,
+        scratch=[
+            pltpu.VMEM(near.shape, near.dtype),
+            pltpu.SemaphoreType.DMA((near.shape[0], 2)),
+        ],
+        input_output_aliases={3: 0},
+    )
+
+
 def body(lesser, greater, couplings, rim_couple, bose_factor, offsets, pattern):
     energies = lax.axis_size("energy")
     cuts = lax.axis_size("cuts")
@@ -364,7 +407,8 @@
     kept = greater_terms(
         scalars, bose_factor, greater, *high, corners, low_kept, couplings, rim_couple
     )
-    return low_out, added(added(kept, core, first), 1 - core, second)
+    later = lax.dynamic_index_in_dim(kept, 1 - core, 0, keepdims=False)[0]
+    return low_out, last_added(place, later, second, added(kept, core, first))
 
 
 def solution(mesh):

time: 110 us -> 110 us (level)
  Pallas kernels: 35.8 us -> 47.3 us
  waiting for transfers between devices: 37.6 us -> 26.9 us
  other arithmetic: 4.97 us -> 2.87 us
    pallas_call x6 -> x7, Pallas kernels: 35.8 us -> 47.3 us  [call(): pl.pallas_call(kernel, grid_spec=pltpu.PrefetchScalarGridSpec(num_scalar_...]
    ppermute x6, waiting for transfers between devices: 37.5 us -> 26.9 us  [shifted(): return lax.ppermute(x, ('energy', 'cuts'), pairs)]
    ppermute x6, starting transfers between devices: 23.8 us -> 26.3 us  [shifted(): return lax.ppermute(x, ('energy', 'cuts'), pairs)]
    ppermute x2, starting transfers between devices: 4.65 us -> 2.12 us  [swapped(): return lax.ppermute(x, ('energy', 'cuts'), pairs)]
    dynamic_update_slice x2 -> x1, other arithmetic: 4.97 us -> 2.87 us  [added(): return lax.dynamic_update_slice_in_dim(near, slab, at, 0)]
  transfers between devices with their start and end apart: 8 -> 8, of which waited for: 4 -> 4; matrix products, arithmetic and copies ran while one was open for 3% -> 4% of each run, Pallas kernels for 31% -> 41%
where the time goes in v3:
time: 110 us; the launch traced here: 108 us
  Pallas kernels  47.3 us (43%)
  starting transfers between devices  28.4 us (26%)
  waiting for transfers between devices  26.9 us (24%)
  other arithmetic  2.87 us (3%)
  local copies, waits for them, and re-layouts  1.49 us (1%)
    pallas_call x7, Pallas kernels, call(): pl.pallas_call(kernel, grid_spec=pltpu.PrefetchScalarGridSpec(num_scalar_...  47.3 us
    ppermute x6, waiting for transfers between devices, shifted(): return lax.ppermute(x, ('energy', 'cuts'), pairs)  26.9 us
    ppermute x6, starting transfers between devices, shifted(): return lax.ppermute(x, ('energy', 'cuts'), pairs)  26.3 us
    dynamic_update_slice x1, other arithmetic, added(): return lax.dynamic_update_slice_in_dim(near, slab, at, 0)  2.87 us
  transfers between devices with their start and end apart: 8, of which 4 were waited for; matrix products, arithmetic and copies ran while one was open for 4% of the time, Pallas kernels for 41%

profile of v3, /device:TPU:110, one launch (start us, length us, event | category | flops | bytes accessed | tf_op | source)
XLA Modules:
  0.0 107.9 jit_solution(17219361100288563452)
XLA Ops:
  0.6 1.9 %cornered.2 = bf16[2,2,2,128,128]{4,3,2,1,0:T(8,128)(2,1)} custom-call(bf16[2,1,2,512,512]{4,3,2,1,0:T(8,128)(2,1)} %own.2, bf16[2,1,2,512,512]{4,3,2,1,0:T(8,128)(2,1)} %own.3, bf16[2,1,2,512,512]{4,3,2,1,0:T(8,128)(2,1)} %own.2, bf16[2,1,2,512,512]{4,3,2,1,0:T(8,128)(2,1)} %own.3), custom_call_target="tpu_custom_call" | custom-call | bytes 4194304 | tf_op jit(solution)/shard_map/cornered/pallas_call | solution.py:40
  2.5 1.4 %collective-permute-start = (bf16[2,2,2,128,128]{4,3,2,1,0:T(8,128)(2,1)}, bf16[2,2,2,128,128]{4,3,2,1,0:T(8,128)(2,1)}, u32[]{:S(2)}, u32[]{:S(2)}) collective-permute-start(bf16[2,2,2,128,128]{4,3,2,1,0:T(8,128)(2,1)} %cornered.2), channel_id=1, source_target_pairs={{1,2},{2,1},{5,6},{6,5},{9,10},{10,9},{13,14},{14,13},{17,18},{18,... | collective-permute-start | bytes 786440 | tf_op jit(solution)/shard_map/ppermute | solution.py:27
  3.9 0.5 placed.1.place
  4.4 4.8 %collective-permute-start.1 = (bf16[2,1,2,512,512]{4,3,2,1,0:T(8,128)(2,1)}, bf16[2,1,2,512,512]{4,3,2,1,0:T(8,128)(2,1)}, u32[]{:S(2)}, u32[]{:S(2)}) collective-permute-start(bf16[2,1,2,512,512]{4,3,2,1,0:T(8,128)(2,1)} %own.2), channel_id=1, source_target_pairs={{0,4},{2,6},{4,8},{5,1},{6,10},{7,3},{8,12},{9,5},{10,14},{11,7},{... | collective-permute-start | bytes 6291464 | tf_op jit(solution)/shard_map/ppermute | solution.py:17
  9.3 1.9 %collective-permute-start.2 = (bf16[2,1,2,512,512]{4,3,2,1,0:T(8,128)(2,1)}, bf16[2,1,2,512,512]{4,3,2,1,0:T(8,128)(2,1)}, u32[]{:S(2)}, u32[]{:S(2)}) collective-permute-start(bf16[2,1,2,512,512]{4,3,2,1,0:T(8,128)(2,1)} %own.2), channel_id=1, source_target_pairs={{1,5},{3,7},{4,0},{5,9},{6,2},{7,11},{8,4},{9,13},{10,6},{11,15},{... | collective-permute-start | bytes 6291464 | tf_op jit(solution)/shard_map/ppermute | solution.py:17
  11.2 0.0 collective-permute-done.outer
  11.2 11.4 %far_terms.1 = (bf16[2,512,512]{2,1,0:T(8,128)(2,1)}, bf16[2,512,512]{2,1,0:T(8,128)(2,1)}) custom-call(s32[2]{0:T(128)} %placed.1.place, s32[3]{0:T(128)} %offsets.5, s32[4,3]{1,0:T(4,128)} %pattern.5, f32[3]{0:T(128)} %bose.5, bf16[2,1,2,512,512]{4,3,2,1,0:T(8,128)(2,1)} %own.3, bf16[1,3,512,512]{3,2,1,0:T(8,128)(2,1)} %couple.5), custom_call_target="tpu_custom_call" | custom-call | flops 25769803776 | bytes 4194304 | tf_op jit(solution)/shard_map/far_terms/pallas_call | solution.py:40
  22.6 0.0 copy-start.1
  22.6 2.0 %cornered.3 = bf16[2,2,2,128,128]{4,3,2,1,0:T(8,128)(2,1)} custom-call(bf16[2,1,2,512,512]{4,3,2,1,0:T(8,128)(2,1)} %own.2, bf16[2,1,2,512,512]{4,3,2,1,0:T(8,128)(2,1)} %own.3, bf16[2,1,2,512,512]{4,3,2,1,0:T(8,128)(2,1)} %own.2, bf16[2,1,2,512,512]{4,3,2,1,0:T(8,128)(2,1)} %own.3), custom_call_target="tpu_custom_call" | custom-call | bytes 4194304 | tf_op jit(solution)/shard_map/cornered/pallas_call | solution.py:40
  24.7 0.8 collective-permute-start.3
  25.4 0.0 copy-done.1
  25.4 0.0 copy-start.2
  25.4 1.5 %constant_dynamic-slice_fusion = (bf16[1,1,2,512,512]{4,3,2,1,0:T(8,128)(2,1)}, bf16[1,1,2,512,512]{4,3,2,1,0:T(8,128)(2,1)}) fusion(bf16[2,1,2,512,512]{4,3,2,1,0:T(8,128)(2,1)S(1)} %copy-done.1, s32[]{:T(128)S(6)} %select_n.12, s32[]{:T(128)S(6)} %select_n.11), kind=kLoop, calls=%fused_computation.4 | loop fusion | bytes 4194312 | tf_op jit(solution)/shard_map/dynamic_slice | solution.py:390
  26.9 7.4 %collective-permute-start.4 = (bf16[1,1,2,512,512]{4,3,2,1,0:T(8,128)(2,1)}, bf16[1,1,2,512,512]{4,3,2,1,0:T(8,128)(2,1)}, u32[]{:S(2)}, u32[]{:S(2)}) collective-permute-start(bf16[1,1,2,512,512]{4,3,2,1,0:T(8,128)(2,1)} %get-tuple-element.35), channel_id=1, source_target_pairs={{0,4},{2,6},{4,8},{5,1},{6,10},{7,3},{8,12},{9,5},{10,14},{11,7},{... | collective-permute-start | bytes 3145736 | tf_op jit(solution)/shard_map/ppermute | solution.py:17
  34.3 1.9 %collective-permute-start.5 = (bf16[1,1,2,512,512]{4,3,2,1,0:T(8,128)(2,1)}, bf16[1,1,2,512,512]{4,3,2,1,0:T(8,128)(2,1)}, u32[]{:S(2)}, u32[]{:S(2)}) collective-permute-start(bf16[1,1,2,512,512]{4,3,2,1,0:T(8,128)(2,1)} %get-tuple-element.34), channel_id=1, source_target_pairs={{1,5},{3,7},{4,0},{5,9},{6,2},{7,11},{8,4},{9,13},{10,6},{11,15},{... | collective-permute-start | bytes 3145736 | tf_op jit(solution)/shard_map/ppermute | solution.py:17
  36.2 0.0 collective-permute-done.3.inner
  36.2 0.0 copy-start.3
  36.3 8.1 %collective-permute-start.7 = (bf16[2,512,512]{2,1,0:T(8,128)(2,1)}, bf16[2,512,512]{2,1,0:T(8,128)(2,1)S(1)}, u32[]{:S(2)}, u32[]{:S(2)}) collective-permute-start(bf16[2,512,512]{2,1,0:T(8,128)(2,1)} %get-tuple-element.31), channel_id=1, source_target_pairs={{0,4},{2,6},{4,8},{5,1},{6,10},{7,3},{8,12},{9,5},{10,14},{11,7},{... | collective-permute-start | bytes 3145736 | tf_op jit(solution)/shard_map/ppermute | solution.py:17
  44.4 6.2 %collective-permute-done.1.first = bf16[2,1,2,512,512]{4,3,2,1,0:T(8,128)(2,1)} collective-permute-done((bf16[2,1,2,512,512]{4,3,2,1,0:T(8,128)(2,1)}, bf16[2,1,2,512,512]{4,3,2,1,0:T(8,128)(2,1)}, u32[]{:S(2)}, u32[]{:S(2)}) %collective-permute-start.1) | collective-permute-done | bytes 2097184 | tf_op jit(solution)/shard_map/ppermute | solution.py:17
  50.6 13.7 %collective-permute-done.2.second = bf16[2,1,2,512,512]{4,3,2,1,0:T(8,128)(2,1)} collective-permute-done((bf16[2,1,2,512,512]{4,3,2,1,0:T(8,128)(2,1)}, bf16[2,1,2,512,512]{4,3,2,1,0:T(8,128)(2,1)}, u32[]{:S(2)}, u32[]{:S(2)}) %collective-permute-start.2) | collective-permute-done | bytes 2097184 | tf_op jit(solution)/shard_map/ppermute | solution.py:17
  64.3 0.0 copy-done.2
  64.3 2.1 %collective-permute-start.6 = (bf16[2,512,512]{2,1,0:T(8,128)(2,1)S(1)}, bf16[2,512,512]{2,1,0:T(8,128)(2,1)S(1)}, u32[]{:S(2)}, u32[]{:S(2)}) collective-permute-start(bf16[2,512,512]{2,1,0:T(8,128)(2,1)S(1)} %copy-done.2), channel_id=1, source_target_pairs={{1,5},{3,7},{4,0},{5,9},{6,2},{7,11},{8,4},{9,13},{10,6},{11,15},{... | collective-permute-start | bytes 3145736 | tf_op jit(solution)/shard_map/ppermute | solution.py:17
  66.4 0.0 copy-done.3
  66.4 15.3 %lesser_terms.1 = (bf16[2,1,2,512,512]{4,3,2,1,0:T(8,128)(2,1)}, f32[2,2,512,512]{3,2,1,0:T(8,128)}) custom-call(s32[2]{0:T(128)} %placed.1.place, s32[3]{0:T(128)} %offsets.5, s32[4,3]{1,0:T(4,128)} %pattern.5, f32[3]{0:T(128)} %bose.5, bf16[2,1,2,512,512]{4,3,2,1,0:T(8,128)(2,1)} %own.2, bf16[2,1,2,512,512]{4,3,2,1,0:T(8,128)(2,1)} %collective-permute-done.1.first, ...), custom_call_target="tpu_custom_call" | custom-call | flops 12884901888 | bytes 4194304 | tf_op jit(solution)/shard_map/lesser_terms/pallas_call | solution.py:40
  81.7 0.0 collective-permute-done.4.first
  81.7 5.1 %collective-permute-done.5.second = bf16[1,1,2,512,512]{4,3,2,1,0:T(8,128)(2,1)} collective-permute-done((bf16[1,1,2,512,512]{4,3,2,1,0:T(8,128)(2,1)}, bf16[1,1,2,512,512]{4,3,2,1,0:T(8,128)(2,1)}, u32[]{:S(2)}, u32[]{:S(2)}) %collective-permute-start.5) | collective-permute-done | bytes 1048608 | tf_op jit(solution)/shard_map/ppermute | solution.py:17
  86.7 14.6 %greater_terms.1 = bf16[2,1,2,512,512]{4,3,2,1,0:T(8,128)(2,1)} custom-call(s32[2]{0:T(128)} %placed.1.place, s32[3]{0:T(128)} %offsets.5, s32[4,3]{1,0:T(4,128)} %pattern.5, f32[3]{0:T(128)} %bose.5, bf16[2,1,2,512,512]{4,3,2,1,0:T(8,128)(2,1)} %own.3, bf16[1,1,2,512,512]{4,3,2,1,0:T(8,128)(2,1)} %collective-permute-done.4.first, ...), custom_call_target="tpu_custom_call" | custom-call | flops 12884901888 | bytes 4194304 | tf_op jit(solution)/shard_map/greater_terms/pallas_call | solution.py:40
  101.3 0.0 copy-start
  101.3 0.0 collective-permute-done.7
  101.3 2.9 %fusion.1 = (bf16[2,1,2,512,512]{4,3,2,1,0:T(8,128)(2,1)}, bf16[2,512,512]{2,1,0:T(8,128)(2,1)S(1)}) fusion(bf16[2,1,2,512,512]{4,3,2,1,0:T(8,128)(2,1)} %greater_terms.1, s32[]{:T(128)S(6)} %select_n.12, bf16[2,512,512]{2,1,0:T(8,128)(2,1)S(1)} %collective-permute-done.7, s32[]{:T(128)S(6)} %select_n.11), kind=kLoop, calls=%fused_computation.2 | loop fusion | flops 2097152 | bytes 5242888 | tf_op jit(solution)/shard_map/dynamic_update_slice | solution.py:335
  104.2 2.0 %collective-permute-done.6.far = bf16[2,512,512]{2,1,0:T(8,128)(2,1)S(1)} collective-permute-done((bf16[2,512,512]{2,1,0:T(8,128)(2,1)S(1)}, bf16[2,512,512]{2,1,0:T(8,128)(2,1)S(1)}, u32[]{:S(2)}, u32[]{:S(2)}) %collective-permute-start.6) | collective-permute-done | bytes 1048608 | tf_op jit(solution)/shard_map/ppermute | solution.py:17
  106.2 0.0 copy-done
  106.2 1.6 %last_added.1 = bf16[2,1,2,512,512]{4,3,2,1,0:T(8,128)(2,1)} custom-call(s32[2]{0:T(128)S(1)} %copy-done, bf16[2,512,512]{2,1,0:T(8,128)(2,1)S(1)} %get-tuple-element.33.near, bf16[2,512,512]{2,1,0:T(8,128)(2,1)S(1)} %collective-permute-done.6.far, bf16[2,1,2,512,512]{4,3,2,1,0:T(8,128)(2,1)} %get-tuple-element.32.partial), custom_call_target="tpu_custom_call", output_to_operand_aliasing={{}: (3, {})} | custom-call | flops 1000000000 | bytes 4194304 | tf_op jit(solution)/shard_map/last_added/pallas_call | solution.py:40
Async XLA Ops:
  2.5 8.7 %collective-permute-start = (bf16[2,2,2,128,128]{4,3,2,1,0:T(8,128)(2,1)}, bf16[2,2,2,128,128]{4,3,2,1,0:T(8,128)(2,1)}, u32[]{:S(2)}, u32[]{:S(2)}) collective-permute-start(bf16[2,2,2,128,128]{4,3,2,1,0:T(8,128)(2,1)} %cornered.2), channel_id=1, source_target_pairs={{1,2},{2,1},{5,6},{6,5},{9,10},{10,9},{13,14},{14,13},{17,18},{18,... | collective-permute-start | bytes 786440 | tf_op jit(solution)/shard_map/ppermute | solution.py:27
  4.4 46.2 %collective-permute-start.1 = (bf16[2,1,2,512,512]{4,3,2,1,0:T(8,128)(2,1)}, bf16[2,1,2,512,512]{4,3,2,1,0:T(8,128)(2,1)}, u32[]{:S(2)}, u32[]{:S(2)}) collective-permute-start(bf16[2,1,2,512,512]{4,3,2,1,0:T(8,128)(2,1)} %own.2), channel_id=1, source_target_pairs={{0,4},{2,6},{4,8},{5,1},{6,10},{7,3},{8,12},{9,5},{10,14},{11,7},{... | collective-permute-start | bytes 6291464 | tf_op jit(solution)/shard_map/ppermute | solution.py:17
  9.3 55.0 %collective-permute-start.2 = (bf16[2,1,2,512,512]{4,3,2,1,0:T(8,128)(2,1)}, bf16[2,1,2,512,512]{4,3,2,1,0:T(8,128)(2,1)}, u32[]{:S(2)}, u32[]{:S(2)}) collective-permute-start(bf16[2,1,2,512,512]{4,3,2,1,0:T(8,128)(2,1)} %own.2), channel_id=1, source_target_pairs={{1,5},{3,7},{4,0},{5,9},{6,2},{7,11},{8,4},{9,13},{10,6},{11,15},{... | collective-permute-start | bytes 6291464 | tf_op jit(solution)/shard_map/ppermute | solution.py:17
  22.6 2.8 %copy-start.1 = (bf16[2,1,2,512,512]{4,3,2,1,0:T(8,128)(2,1)S(1)}, bf16[2,1,2,512,512]{4,3,2,1,0:T(8,128)(2,1)}, u32[]{:S(2)}) copy-start(bf16[2,1,2,512,512]{4,3,2,1,0:T(8,128)(2,1)} %own.3) | copy-start | bytes 6291460
  24.7 11.6 %collective-permute-start.3 = (bf16[2,2,2,128,128]{4,3,2,1,0:T(8,128)(2,1)}, bf16[2,2,2,128,128]{4,3,2,1,0:T(8,128)(2,1)S(1)}, u32[]{:S(2)}, u32[]{:S(2)}) collective-permute-start(bf16[2,2,2,128,128]{4,3,2,1,0:T(8,128)(2,1)} %cornered.3), channel_id=1, source_target_pairs={{0,1},{1,0},{2,3},{3,2},{4,5},{5,4},{6,7},{7,6},{8,9},{9,8},{10,11... | collective-permute-start | bytes 786440 | tf_op jit(solution)/shard_map/ppermute | solution.py:27
  25.4 38.8 %copy-start.2 = (bf16[2,512,512]{2,1,0:T(8,128)(2,1)S(1)}, bf16[2,512,512]{2,1,0:T(8,128)(2,1)}, u32[]{:S(2)}) copy-start(bf16[2,512,512]{2,1,0:T(8,128)(2,1)} %get-tuple-element.30) | copy-start | bytes 3145732
  26.9 54.8 %collective-permute-start.4 = (bf16[1,1,2,512,512]{4,3,2,1,0:T(8,128)(2,1)}, bf16[1,1,2,512,512]{4,3,2,1,0:T(8,128)(2,1)}, u32[]{:S(2)}, u32[]{:S(2)}) collective-permute-start(bf16[1,1,2,512,512]{4,3,2,1,0:T(8,128)(2,1)} %get-tuple-element.35), channel_id=1, source_target_pairs={{0,4},{2,6},{4,8},{5,1},{6,10},{7,3},{8,12},{9,5},{10,14},{11,7},{... | collective-permute-start | bytes 3145736 | tf_op jit(solution)/shard_map/ppermute | solution.py:17
  34.3 52.4 %collective-permute-start.5 = (bf16[1,1,2,512,512]{4,3,2,1,0:T(8,128)(2,1)}, bf16[1,1,2,512,512]{4,3,2,1,0:T(8,128)(2,1)}, u32[]{:S(2)}, u32[]{:S(2)}) collective-permute-start(bf16[1,1,2,512,512]{4,3,2,1,0:T(8,128)(2,1)} %get-tuple-element.34), channel_id=1, source_target_pairs={{1,5},{3,7},{4,0},{5,9},{6,2},{7,11},{8,4},{9,13},{10,6},{11,15},{... | collective-permute-start | bytes 3145736 | tf_op jit(solution)/shard_map/ppermute | solution.py:17
  36.2 30.1 %copy-start.3 = (bf16[2,2,2,128,128]{4,3,2,1,0:T(8,128)(2,1)}, bf16[2,2,2,128,128]{4,3,2,1,0:T(8,128)(2,1)S(1)}, u32[]{:S(2)}) copy-start(bf16[2,2,2,128,128]{4,3,2,1,0:T(8,128)(2,1)S(1)} %collective-permute-done.3.inner) | copy-start | bytes 786436
  36.3 65.1 %collective-permute-start.7 = (bf16[2,512,512]{2,1,0:T(8,128)(2,1)}, bf16[2,512,512]{2,1,0:T(8,128)(2,1)S(1)}, u32[]{:S(2)}, u32[]{:S(2)}) collective-permute-start(bf16[2,512,512]{2,1,0:T(8,128)(2,1)} %get-tuple-element.31), channel_id=1, source_target_pairs={{0,4},{2,6},{4,8},{5,1},{6,10},{7,3},{8,12},{9,5},{10,14},{11,7},{... | collective-permute-start | bytes 3145736 | tf_op jit(solution)/shard_map/ppermute | solution.py:17
  64.3 41.9 %collective-permute-start.6 = (bf16[2,512,512]{2,1,0:T(8,128)(2,1)S(1)}, bf16[2,512,512]{2,1,0:T(8,128)(2,1)S(1)}, u32[]{:S(2)}, u32[]{:S(2)}) collective-permute-start(bf16[2,512,512]{2,1,0:T(8,128)(2,1)S(1)} %copy-done.2), channel_id=1, source_target_pairs={{1,5},{3,7},{4,0},{5,9},{6,2},{7,11},{8,4},{9,13},{10,6},{11,15},{... | collective-permute-start | bytes 3145736 | tf_op jit(solution)/shard_map/ppermute | solution.py:17
  101.3 4.9 %copy-start = (s32[2]{0:T(128)S(1)}, s32[2]{0:T(128)}, u32[]{:S(2)}) copy-start(s32[2]{0:T(128)} %placed.1.place) | copy-start | bytes 28

commit v4 on v3

--- a/solution.py
+++ b/solution.py
@@ -54,31 +54,36 @@
     )(*scalars, *operands)
 
 
-def corner_kernel(inside, low_top, high_top, low_bottom, high_bottom, out):
+def corner_kernel(inside, width, lesser, greater, out, sems):
     core = lax.axis_index("cuts") & 1
-    for kind, (top, bottom) in enumerate(((low_top, low_bottom), (high_top, high_bottom))):
-        upper = core == 1 if inside else core == 0
-        out[:, kind] = jnp.where(upper, top[:, 0], bottom[:, 0])
+    last = (lesser.shape[-1] - width) // width
+    upper = (1 - core if inside else core) * last
+    edge = pl.ds(pl.multiple_of(upper * width, width), width)
+    copies = [
+        pltpu.make_async_copy(green.at[:, 0, :, edge, edge], out.at[:, kind], sems.at[kind])
+        for kind, green in enumerate((lesser, greater))
+    ]
+    for copy in copies:
+        copy.start()
+    for copy in copies:
+        copy.wait()
 
 
 def cornered(inside, width, lesser, greater):
-    parts = lesser.shape[2]
-    last = lesser.shape[-1] // width - 1
-    shape = (2, 2, parts, width, width)
-    block = (2, 1, parts, width, width)
-    top = pl.BlockSpec(block, lambda i: (0, 0, 0, 0, 0))
-    bottom = pl.BlockSpec(block, lambda i: (0, 0, 0, last, last))
-    return call(
-        lambda *refs: corner_kernel(inside, *refs),
+    shape = (2, 2, lesser.shape[2], width, width)
+    anywhere = pl.BlockSpec(memory_space=pl.ANY)
+    return call(
+        lambda *refs: corner_kernel(inside, width, *refs),
         "cornered",
         (),
-        (lesser, greater, lesser, greater),
-        (1,),
-        [top, top, bottom, bottom],
-        pl.BlockSpec(shape, lambda i: (0, 0, 0, 0, 0)),
+        (lesser, greater),
+        (),
+        [anywhere, anywhere],
+        pl.BlockSpec(memory_space=pltpu.VMEM),
         jax.ShapeDtypeStruct(shape, lesser.dtype),
-        60,
+        58,
         0,
+        scratch=[pltpu.SemaphoreType.DMA((2,))],
     )
 
 
@@ -338,10 +343,10 @@
 def last_kernel(place, near, far, partial, out, mixed, sems):
     energy = 1 - place[1]
     parts, orbitals = mixed.shape[0], mixed.shape[1]
-    rows = orbitals // 2
+    rows = orbitals // 4
     copies = []
     for part in range(parts):
-        for half in range(2):
+        for half in range(4):
             at = slice(half * rows, (half + 1) * rows)
             value = near[part, at].astype(jnp.float32) + far[part, at].astype(jnp.float32)
             mixed[part, at] = value.astype(mixed.dtype)
@@ -372,7 +377,7 @@
         10**9,
         scratch=[
             pltpu.VMEM(near.shape, near.dtype),
-            pltpu.SemaphoreType.DMA((near.shape[0], 2)),
+            pltpu.SemaphoreType.DMA((near.shape[0], 4)),
         ],
         input_output_aliases={3: 0},
     )

time: 110 us -> 110 us (level)
  Pallas kernels: 47.3 us -> 44.6 us
  waiting for transfers between devices: 26.9 us -> 29.3 us
    pallas_call x7, Pallas kernels: 47.3 us -> 44.6 us  [call(): pl.pallas_call(kernel, grid_spec=pltpu.PrefetchScalarGridSpec(num_scalar_...]
    ppermute x2, starting transfers between devices: 2.12 us -> 4.67 us  [swapped(): return lax.ppermute(x, ('energy', 'cuts'), pairs)]
    ppermute x6, starting transfers between devices: 26.3 us -> 23.9 us  [shifted(): return lax.ppermute(x, ('energy', 'cuts'), pairs)]
    ppermute x6, waiting for transfers between devices: 26.9 us -> 29.3 us  [shifted(): return lax.ppermute(x, ('energy', 'cuts'), pairs)]
  transfers between devices with their start and end apart: 8 -> 8, of which waited for: 4 -> 4; matrix products, arithmetic and copies ran while one was open for 4% -> 4% of each run, Pallas kernels for 41% -> 38%
where the time goes in v4:
time: 110 us; the launch traced here: 108 us
  Pallas kernels  44.6 us (41%)
  waiting for transfers between devices  29.3 us (27%)
  starting transfers between devices  28.5 us (26%)
  other arithmetic  2.87 us (3%)
  local copies, waits for them, and re-layouts  1.49 us (1%)
    pallas_call x7, Pallas kernels, call(): pl.pallas_call(kernel, grid_spec=pltpu.PrefetchScalarGridSpec(num_scalar_...  44.6 us
    ppermute x6, waiting for transfers between devices, shifted(): return lax.ppermute(x, ('energy', 'cuts'), pairs)  29.3 us
    ppermute x6, starting transfers between devices, shifted(): return lax.ppermute(x, ('energy', 'cuts'), pairs)  23.9 us
    ppermute x2, starting transfers between devices, swapped(): return lax.ppermute(x, ('energy', 'cuts'), pairs)  4.67 us
    dynamic_update_slice x1, other arithmetic, added(): return lax.dynamic_update_slice_in_dim(near, slab, at, 0)  2.87 us
  transfers between devices with their start and end apart: 8, of which 4 were waited for; matrix products, arithmetic and copies ran while one was open for 4% of the time, Pallas kernels for 38%

profile of v4, /device:TPU:110, one launch (start us, length us, event | category | flops | bytes accessed | tf_op | source)
XLA Modules:
  0.0 107.8 jit_solution(643657396409538911)
XLA Ops:
  0.6 1.7 %cornered.2 = bf16[2,2,2,128,128]{4,3,2,1,0:T(8,128)(2,1)} custom-call(bf16[2,1,2,512,512]{4,3,2,1,0:T(8,128)(2,1)} %own.2, bf16[2,1,2,512,512]{4,3,2,1,0:T(8,128)(2,1)} %own.3), custom_call_target="tpu_custom_call" | custom-call | bytes 4194304 | tf_op jit(solution)/shard_map/cornered/pallas_call | solution.py:40
  2.3 1.4 %collective-permute-start = (bf16[2,2,2,128,128]{4,3,2,1,0:T(8,128)(2,1)}, bf16[2,2,2,128,128]{4,3,2,1,0:T(8,128)(2,1)}, u32[]{:S(2)}, u32[]{:S(2)}) collective-permute-start(bf16[2,2,2,128,128]{4,3,2,1,0:T(8,128)(2,1)} %cornered.2), channel_id=1, source_target_pairs={{1,2},{2,1},{5,6},{6,5},{9,10},{10,9},{13,14},{14,13},{17,18},{18,... | collective-permute-start | bytes 786440 | tf_op jit(solution)/shard_map/ppermute | solution.py:27
  3.7 0.5 placed.1.place
  4.2 4.8 %collective-permute-start.1 = (bf16[2,1,2,512,512]{4,3,2,1,0:T(8,128)(2,1)}, bf16[2,1,2,512,512]{4,3,2,1,0:T(8,128)(2,1)}, u32[]{:S(2)}, u32[]{:S(2)}) collective-permute-start(bf16[2,1,2,512,512]{4,3,2,1,0:T(8,128)(2,1)} %own.2), channel_id=1, source_target_pairs={{0,4},{2,6},{4,8},{5,1},{6,10},{7,3},{8,12},{9,5},{10,14},{11,7},{... | collective-permute-start | bytes 6291464 | tf_op jit(solution)/shard_map/ppermute | solution.py:17
  9.1 1.9 %collective-permute-start.2 = (bf16[2,1,2,512,512]{4,3,2,1,0:T(8,128)(2,1)}, bf16[2,1,2,512,512]{4,3,2,1,0:T(8,128)(2,1)}, u32[]{:S(2)}, u32[]{:S(2)}) collective-permute-start(bf16[2,1,2,512,512]{4,3,2,1,0:T(8,128)(2,1)} %own.2), channel_id=1, source_target_pairs={{1,5},{3,7},{4,0},{5,9},{6,2},{7,11},{8,4},{9,13},{10,6},{11,15},{... | collective-permute-start | bytes 6291464 | tf_op jit(solution)/shard_map/ppermute | solution.py:17
  11.0 0.0 collective-permute-done.outer
  11.0 8.9 %far_terms.1 = (bf16[2,512,512]{2,1,0:T(8,128)(2,1)}, bf16[2,512,512]{2,1,0:T(8,128)(2,1)}) custom-call(s32[2]{0:T(128)} %placed.1.place, s32[3]{0:T(128)} %offsets.5, s32[4,3]{1,0:T(4,128)} %pattern.5, f32[3]{0:T(128)} %bose.5, bf16[2,1,2,512,512]{4,3,2,1,0:T(8,128)(2,1)} %own.3, bf16[1,3,512,512]{3,2,1,0:T(8,128)(2,1)} %couple.5), custom_call_target="tpu_custom_call" | custom-call | flops 25769803776 | bytes 4194304 | tf_op jit(solution)/shard_map/far_terms/pallas_call | solution.py:40
  20.0 0.0 copy-start.1
  20.0 1.8 %cornered.3 = bf16[2,2,2,128,128]{4,3,2,1,0:T(8,128)(2,1)} custom-call(bf16[2,1,2,512,512]{4,3,2,1,0:T(8,128)(2,1)} %own.2, bf16[2,1,2,512,512]{4,3,2,1,0:T(8,128)(2,1)} %own.3), custom_call_target="tpu_custom_call" | custom-call | bytes 4194304 | tf_op jit(solution)/shard_map/cornered/pallas_call | solution.py:40
  21.8 3.3 %collective-permute-start.3 = (bf16[2,2,2,128,128]{4,3,2,1,0:T(8,128)(2,1)}, bf16[2,2,2,128,128]{4,3,2,1,0:T(8,128)(2,1)S(1)}, u32[]{:S(2)}, u32[]{:S(2)}) collective-permute-start(bf16[2,2,2,128,128]{4,3,2,1,0:T(8,128)(2,1)} %cornered.3), channel_id=1, source_target_pairs={{0,1},{1,0},{2,3},{3,2},{4,5},{5,4},{6,7},{7,6},{8,9},{9,8},{10,11... | collective-permute-start | bytes 786440 | tf_op jit(solution)/shard_map/ppermute | solution.py:27
  25.1 0.0 copy-done.1
  25.1 0.0 copy-start.2
  25.1 1.5 %constant_dynamic-slice_fusion = (bf16[1,1,2,512,512]{4,3,2,1,0:T(8,128)(2,1)}, bf16[1,1,2,512,512]{4,3,2,1,0:T(8,128)(2,1)}) fusion(bf16[2,1,2,512,512]{4,3,2,1,0:T(8,128)(2,1)S(1)} %copy-done.1, s32[]{:T(128)S(6)} %select_n.12, s32[]{:T(128)S(6)} %select_n.11), kind=kLoop, calls=%fused_computation.4 | loop fusion | bytes 4194312 | tf_op jit(solution)/shard_map/dynamic_slice | solution.py:395
  26.6 5.0 %collective-permute-start.4 = (bf16[1,1,2,512,512]{4,3,2,1,0:T(8,128)(2,1)}, bf16[1,1,2,512,512]{4,3,2,1,0:T(8,128)(2,1)}, u32[]{:S(2)}, u32[]{:S(2)}) collective-permute-start(bf16[1,1,2,512,512]{4,3,2,1,0:T(8,128)(2,1)} %get-tuple-element.35), channel_id=1, source_target_pairs={{0,4},{2,6},{4,8},{5,1},{6,10},{7,3},{8,12},{9,5},{10,14},{11,7},{... | collective-permute-start | bytes 3145736 | tf_op jit(solution)/shard_map/ppermute | solution.py:17
  31.6 1.9 %collective-permute-start.5 = (bf16[1,1,2,512,512]{4,3,2,1,0:T(8,128)(2,1)}, bf16[1,1,2,512,512]{4,3,2,1,0:T(8,128)(2,1)}, u32[]{:S(2)}, u32[]{:S(2)}) collective-permute-start(bf16[1,1,2,512,512]{4,3,2,1,0:T(8,128)(2,1)} %get-tuple-element.34), channel_id=1, source_target_pairs={{1,5},{3,7},{4,0},{5,9},{6,2},{7,11},{8,4},{9,13},{10,6},{11,15},{... | collective-permute-start | bytes 3145736 | tf_op jit(solution)/shard_map/ppermute | solution.py:17
  33.5 0.0 collective-permute-done.3.inner
  33.5 0.0 copy-start.3
  33.5 8.1 %collective-permute-start.7 = (bf16[2,512,512]{2,1,0:T(8,128)(2,1)}, bf16[2,512,512]{2,1,0:T(8,128)(2,1)S(1)}, u32[]{:S(2)}, u32[]{:S(2)}) collective-permute-start(bf16[2,512,512]{2,1,0:T(8,128)(2,1)} %get-tuple-element.31), channel_id=1, source_target_pairs={{0,4},{2,6},{4,8},{5,1},{6,10},{7,3},{8,12},{9,5},{10,14},{11,7},{... | collective-permute-start | bytes 3145736 | tf_op jit(solution)/shard_map/ppermute | solution.py:17
  41.7 8.8 %collective-permute-done.1.first = bf16[2,1,2,512,512]{4,3,2,1,0:T(8,128)(2,1)} collective-permute-done((bf16[2,1,2,512,512]{4,3,2,1,0:T(8,128)(2,1)}, bf16[2,1,2,512,512]{4,3,2,1,0:T(8,128)(2,1)}, u32[]{:S(2)}, u32[]{:S(2)}) %collective-permute-start.1) | collective-permute-done | bytes 2097184 | tf_op jit(solution)/shard_map/ppermute | solution.py:17
  50.4 13.7 %collective-permute-done.2.second = bf16[2,1,2,512,512]{4,3,2,1,0:T(8,128)(2,1)} collective-permute-done((bf16[2,1,2,512,512]{4,3,2,1,0:T(8,128)(2,1)}, bf16[2,1,2,512,512]{4,3,2,1,0:T(8,128)(2,1)}, u32[]{:S(2)}, u32[]{:S(2)}) %collective-permute-start.2) | collective-permute-done | bytes 2097184 | tf_op jit(solution)/shard_map/ppermute | solution.py:17
  64.1 0.0 copy-done.2
  64.1 2.1 %collective-permute-start.6 = (bf16[2,512,512]{2,1,0:T(8,128)(2,1)S(1)}, bf16[2,512,512]{2,1,0:T(8,128)(2,1)S(1)}, u32[]{:S(2)}, u32[]{:S(2)}) collective-permute-start(bf16[2,512,512]{2,1,0:T(8,128)(2,1)S(1)} %copy-done.2), channel_id=1, source_target_pairs={{1,5},{3,7},{4,0},{5,9},{6,2},{7,11},{8,4},{9,13},{10,6},{11,15},{... | collective-permute-start | bytes 3145736 | tf_op jit(solution)/shard_map/ppermute | solution.py:17
  66.2 0.0 copy-done.3
  66.2 15.3 %lesser_terms.1 = (bf16[2,1,2,512,512]{4,3,2,1,0:T(8,128)(2,1)}, f32[2,2,512,512]{3,2,1,0:T(8,128)}) custom-call(s32[2]{0:T(128)} %placed.1.place, s32[3]{0:T(128)} %offsets.5, s32[4,3]{1,0:T(4,128)} %pattern.5, f32[3]{0:T(128)} %bose.5, bf16[2,1,2,512,512]{4,3,2,1,0:T(8,128)(2,1)} %own.2, bf16[2,1,2,512,512]{4,3,2,1,0:T(8,128)(2,1)} %collective-permute-done.1.first, ...), custom_call_target="tpu_custom_call" | custom-call | flops 12884901888 | bytes 4194304 | tf_op jit(solution)/shard_map/lesser_terms/pallas_call | solution.py:40
  81.5 0.0 collective-permute-done.4.first
  81.5 5.0 %collective-permute-done.5.second = bf16[1,1,2,512,512]{4,3,2,1,0:T(8,128)(2,1)} collective-permute-done((bf16[1,1,2,512,512]{4,3,2,1,0:T(8,128)(2,1)}, bf16[1,1,2,512,512]{4,3,2,1,0:T(8,128)(2,1)}, u32[]{:S(2)}, u32[]{:S(2)}) %collective-permute-start.5) | collective-permute-done | bytes 1048608 | tf_op jit(solution)/shard_map/ppermute | solution.py:17
  86.6 14.7 %greater_terms.1 = bf16[2,1,2,512,512]{4,3,2,1,0:T(8,128)(2,1)} custom-call(s32[2]{0:T(128)} %placed.1.place, s32[3]{0:T(128)} %offsets.5, s32[4,3]{1,0:T(4,128)} %pattern.5, f32[3]{0:T(128)} %bose.5, bf16[2,1,2,512,512]{4,3,2,1,0:T(8,128)(2,1)} %own.3, bf16[1,1,2,512,512]{4,3,2,1,0:T(8,128)(2,1)} %collective-permute-done.4.first, ...), custom_call_target="tpu_custom_call" | custom-call | flops 12884901888 | bytes 4194304 | tf_op jit(solution)/shard_map/greater_terms/pallas_call | solution.py:40
  101.3 0.0 copy-start
  101.3 0.0 collective-permute-done.7
  101.3 2.9 %fusion.1 = (bf16[2,1,2,512,512]{4,3,2,1,0:T(8,128)(2,1)}, bf16[2,512,512]{2,1,0:T(8,128)(2,1)S(1)}) fusion(bf16[2,1,2,512,512]{4,3,2,1,0:T(8,128)(2,1)} %greater_terms.1, s32[]{:T(128)S(6)} %select_n.12, bf16[2,512,512]{2,1,0:T(8,128)(2,1)S(1)} %collective-permute-done.7, s32[]{:T(128)S(6)} %select_n.11), kind=kLoop, calls=%fused_computation.2 | loop fusion | flops 2097152 | bytes 5242888 | tf_op jit(solution)/shard_map/dynamic_update_slice | solution.py:340
  104.2 1.8 %collective-permute-done.6.far = bf16[2,512,512]{2,1,0:T(8,128)(2,1)S(1)} collective-permute-done((bf16[2,512,512]{2,1,0:T(8,128)(2,1)S(1)}, bf16[2,512,512]{2,1,0:T(8,128)(2,1)S(1)}, u32[]{:S(2)}, u32[]{:S(2)}) %collective-permute-start.6) | collective-permute-done | bytes 1048608 | tf_op jit(solution)/shard_map/ppermute | solution.py:17
  106.0 0.0 copy-done
  106.0 1.6 %last_added.1 = bf16[2,1,2,512,512]{4,3,2,1,0:T(8,128)(2,1)} custom-call(s32[2]{0:T(128)S(1)} %copy-done, bf16[2,512,512]{2,1,0:T(8,128)(2,1)S(1)} %get-tuple-element.33.near, bf16[2,512,512]{2,1,0:T(8,128)(2,1)S(1)} %collective-permute-done.6.far, bf16[2,1,2,512,512]{4,3,2,1,0:T(8,128)(2,1)} %get-tuple-element.32.partial), custom_call_target="tpu_custom_call", output_to_operand_aliasing={{}: (3, {})} | custom-call | flops 1000000000 | bytes 4194304 | tf_op jit(solution)/shard_map/last_added/pallas_call | solution.py:40
Async XLA Ops:
  2.3 8.7 %collective-permute-start = (bf16[2,2,2,128,128]{4,3,2,1,0:T(8,128)(2,1)}, bf16[2,2,2,128,128]{4,3,2,1,0:T(8,128)(2,1)}, u32[]{:S(2)}, u32[]{:S(2)}) collective-permute-start(bf16[2,2,2,128,128]{4,3,2,1,0:T(8,128)(2,1)} %cornered.2), channel_id=1, source_target_pairs={{1,2},{2,1},{5,6},{6,5},{9,10},{10,9},{13,14},{14,13},{17,18},{18,... | collective-permute-start | bytes 786440 | tf_op jit(solution)/shard_map/ppermute | solution.py:27
  4.2 46.2 %collective-permute-start.1 = (bf16[2,1,2,512,512]{4,3,2,1,0:T(8,128)(2,1)}, bf16[2,1,2,512,512]{4,3,2,1,0:T(8,128)(2,1)}, u32[]{:S(2)}, u32[]{:S(2)}) collective-permute-start(bf16[2,1,2,512,512]{4,3,2,1,0:T(8,128)(2,1)} %own.2), channel_id=1, source_target_pairs={{0,4},{2,6},{4,8},{5,1},{6,10},{7,3},{8,12},{9,5},{10,14},{11,7},{... | collective-permute-start | bytes 6291464 | tf_op jit(solution)/shard_map/ppermute | solution.py:17
  9.1 55.0 %collective-permute-start.2 = (bf16[2,1,2,512,512]{4,3,2,1,0:T(8,128)(2,1)}, bf16[2,1,2,512,512]{4,3,2,1,0:T(8,128)(2,1)}, u32[]{:S(2)}, u32[]{:S(2)}) collective-permute-start(bf16[2,1,2,512,512]{4,3,2,1,0:T(8,128)(2,1)} %own.2), channel_id=1, source_target_pairs={{1,5},{3,7},{4,0},{5,9},{6,2},{7,11},{8,4},{9,13},{10,6},{11,15},{... | collective-permute-start | bytes 6291464 | tf_op jit(solution)/shard_map/ppermute | solution.py:17
  20.0 5.1 %copy-start.1 = (bf16[2,1,2,512,512]{4,3,2,1,0:T(8,128)(2,1)S(1)}, bf16[2,1,2,512,512]{4,3,2,1,0:T(8,128)(2,1)}, u32[]{:S(2)}) copy-start(bf16[2,1,2,512,512]{4,3,2,1,0:T(8,128)(2,1)} %own.3) | copy-start | bytes 6291460
  21.8 11.7 %collective-permute-start.3 = (bf16[2,2,2,128,128]{4,3,2,1,0:T(8,128)(2,1)}, bf16[2,2,2,128,128]{4,3,2,1,0:T(8,128)(2,1)S(1)}, u32[]{:S(2)}, u32[]{:S(2)}) collective-permute-start(bf16[2,2,2,128,128]{4,3,2,1,0:T(8,128)(2,1)} %cornered.3), channel_id=1, source_target_pairs={{0,1},{1,0},{2,3},{3,2},{4,5},{5,4},{6,7},{7,6},{8,9},{9,8},{10,11... | collective-permute-start | bytes 786440 | tf_op jit(solution)/shard_map/ppermute | solution.py:27
  25.1 39.0 %copy-start.2 = (bf16[2,512,512]{2,1,0:T(8,128)(2,1)S(1)}, bf16[2,512,512]{2,1,0:T(8,128)(2,1)}, u32[]{:S(2)}) copy-start(bf16[2,512,512]{2,1,0:T(8,128)(2,1)} %get-tuple-element.30) | copy-start | bytes 3145732
  26.6 54.9 %collective-permute-start.4 = (bf16[1,1,2,512,512]{4,3,2,1,0:T(8,128)(2,1)}, bf16[1,1,2,512,512]{4,3,2,1,0:T(8,128)(2,1)}, u32[]{:S(2)}, u32[]{:S(2)}) collective-permute-start(bf16[1,1,2,512,512]{4,3,2,1,0:T(8,128)(2,1)} %get-tuple-element.35), channel_id=1, source_target_pairs={{0,4},{2,6},{4,8},{5,1},{6,10},{7,3},{8,12},{9,5},{10,14},{11,7},{... | collective-permute-start | bytes 3145736 | tf_op jit(solution)/shard_map/ppermute | solution.py:17
  31.6 55.0 %collective-permute-start.5 = (bf16[1,1,2,512,512]{4,3,2,1,0:T(8,128)(2,1)}, bf16[1,1,2,512,512]{4,3,2,1,0:T(8,128)(2,1)}, u32[]{:S(2)}, u32[]{:S(2)}) collective-permute-start(bf16[1,1,2,512,512]{4,3,2,1,0:T(8,128)(2,1)} %get-tuple-element.34), channel_id=1, source_target_pairs={{1,5},{3,7},{4,0},{5,9},{6,2},{7,11},{8,4},{9,13},{10,6},{11,15},{... | collective-permute-start | bytes 3145736 | tf_op jit(solution)/shard_map/ppermute | solution.py:17
  33.5 32.7 %copy-start.3 = (bf16[2,2,2,128,128]{4,3,2,1,0:T(8,128)(2,1)}, bf16[2,2,2,128,128]{4,3,2,1,0:T(8,128)(2,1)S(1)}, u32[]{:S(2)}) copy-start(bf16[2,2,2,128,128]{4,3,2,1,0:T(8,128)(2,1)S(1)} %collective-permute-done.3.inner) | copy-start | bytes 786436
  33.5 67.8 %collective-permute-start.7 = (bf16[2,512,512]{2,1,0:T(8,128)(2,1)}, bf16[2,512,512]{2,1,0:T(8,128)(2,1)S(1)}, u32[]{:S(2)}, u32[]{:S(2)}) collective-permute-start(bf16[2,512,512]{2,1,0:T(8,128)(2,1)} %get-tuple-element.31), channel_id=1, source_target_pairs={{0,4},{2,6},{4,8},{5,1},{6,10},{7,3},{8,12},{9,5},{10,14},{11,7},{... | collective-permute-start | bytes 3145736 | tf_op jit(solution)/shard_map/ppermute | solution.py:17
  64.1 41.9 %collective-permute-start.6 = (bf16[2,512,512]{2,1,0:T(8,128)(2,1)S(1)}, bf16[2,512,512]{2,1,0:T(8,128)(2,1)S(1)}, u32[]{:S(2)}, u32[]{:S(2)}) collective-permute-start(bf16[2,512,512]{2,1,0:T(8,128)(2,1)S(1)} %copy-done.2), channel_id=1, source_target_pairs={{1,5},{3,7},{4,0},{5,9},{6,2},{7,11},{8,4},{9,13},{10,6},{11,15},{... | collective-permute-start | bytes 3145736 | tf_op jit(solution)/shard_map/ppermute | solution.py:17
  101.3 4.7 %copy-start = (s32[2]{0:T(128)S(1)}, s32[2]{0:T(128)}, u32[]{:S(2)}) copy-start(s32[2]{0:T(128)} %placed.1.place) | copy-start | bytes 28
